TPU v7x, 32 devices: a whole 2x2x4 slice. The times are simulated.
32 devices in a mesh: tile: 8 (over z, core), offs: 4 (over y, x).
Axes of the slice: x: 2, y: 2, z: 4, core: 2. Of those that a mesh axis runs over, the one named last changes fastest.
Arguments:
- traces: float32 [4, 64, 2, 2000], P('offs', 'tile'), may hold values from -6 to 6
- src_node: int32 [4, 64], P('offs', 'tile'), may hold values from 0 to 31
- rec_node: int32 [4, 64, 2], P('offs', 'tile'), may hold values from 0 to 31
- aperture: int32 [4, 64, 2], P('offs', 'tile'), may hold values from 0 to 7, all different within a row; in each aligned block of 8 rows (0 to 7, 8 to 15, ..., all dimensions but the last counted through in order) at most 3 rows name the same one
- time_table: int32 [32, 8, 2048], P(None, 'tile'), may hold values from 0 to 999
- amp_table: float32 [32, 8, 2048], P(None, 'tile'), may hold values from 0.05 to 0.5
- width_table: int32 [32, 8, 2048], P(None, 'tile'), may hold values from 0 to 2
Outputs:
- gathers: float32 [8, 16, 4, 128], P('tile', 'offs')
Inputs may be any that keep to these rules, and one draw needn't show every extreme that they name: `aperture`: each row names 2 different image tiles. Among the 8 rows of one device (aligned blocks of rows in the order offset class, block), no tile is named more than 3 times, a bound that some block reaches.
All inputs are finite; a program needn't handle non-finite values.
Results may differ from a plain program's by a relative error of at most 0.0003.
Values sent between devices are 32-bit elements; how exact they have to be, the bound alone decides.
No kernel may reach another device: no remote copies, remote signals or barrier semaphores. Data moves between devices by JAX's collectives and lax.ppermute only.
A program may use at most 64 MiB of HBM per device.

v0:
```python
import math

import jax
import jax.numpy as jnp
from jax import lax
from jax.sharding import PartitionSpec as P

CELLS = 128
DEPTH = 16


HALF_WIDTHS = (1, 2, 4)


def triangle(signal):
    length = signal.shape[-1]
    last_axis = signal.ndim - 1
    layers = []
    for halfwidth in HALF_WIDTHS:
        padded = jnp.pad(signal, [(0, 0)] * last_axis + [(halfwidth, halfwidth)])
        summed = jnp.zeros(signal.shape, signal.dtype)
        for offset in range(-halfwidth, halfwidth + 1):
            factor = float(halfwidth + 1 - abs(offset)) / float((halfwidth + 1) ** 2)
            summed = summed + factor * lax.slice_in_dim(
                padded, halfwidth + offset, halfwidth + offset + length, axis=last_axis
            )
        layers.append(summed)
    return jnp.stack(layers, axis=-2)


def spread(filtered, sources, receivers, live, time_rows, amp_rows, width_rows):
    samples = filtered.shape[-1]
    source_time = jnp.take(time_rows, sources, axis=0)[:, None, :]
    index_time = source_time + jnp.take(time_rows, receivers, axis=0)
    width_class = jnp.maximum(
        jnp.take(width_rows, sources, axis=0)[:, None, :], jnp.take(width_rows, receivers, axis=0)
    )
    weight = (
        jnp.take(amp_rows, sources, axis=0)[:, None, :]
        * jnp.take(amp_rows, receivers, axis=0)
        * live[:, None, None]
    )
    flat = filtered.reshape(filtered.shape[0] * filtered.shape[1], -1)
    column = (width_class * samples + index_time).reshape(flat.shape[0], -1)
    picked = jnp.take_along_axis(flat, column, axis=1)
    return jnp.sum(weight.reshape(picked.shape) * picked, axis=0)


def body(traces, src_node, rec_node, aperture, time_table, amp_table, width_table):
    tiles = lax.axis_size("tile")
    blocks = traces.shape[1]
    per_block = traces.shape[2]
    samples = traces.shape[3]
    listed = aperture.shape[2]
    capacity = (3 * blocks * listed + 2 * tiles - 1) // (2 * tiles)
    slots = tiles * capacity
    targets = aperture[0].reshape(-1)
    entries = targets.shape[0]
    owner_block = jnp.arange(entries, dtype=jnp.int32) // listed
    tile_hits = (targets[:, None] == jnp.arange(tiles, dtype=jnp.int32)[None, :]).astype(jnp.int32)
    earlier = jnp.cumsum(tile_hits, axis=0) - tile_hits
    position = targets * capacity + jnp.sum(earlier * tile_hits, axis=1)
    slot_hits = (jnp.arange(slots, dtype=jnp.int32)[:, None] == position[None, :]).astype(
        jnp.float32
    )
    block_hits = (owner_block[:, None] == jnp.arange(blocks, dtype=jnp.int32)[None, :]).astype(
        jnp.float32
    )
    selector = jnp.dot(slot_hits, block_hits, precision=lax.Precision.HIGHEST)
    node_ids = (
        jnp.concatenate([src_node[0][:, None], rec_node[0]], axis=1).astype(jnp.float32) + 1.0
    )
    metadata = jnp.dot(selector, node_ids, precision=lax.Precision.HIGHEST).reshape(
        tiles, capacity, per_block + 1
    )
    payload = jnp.dot(selector, traces[0].reshape(blocks, -1), precision=lax.Precision.HIGHEST)
    payload = payload.reshape(tiles, capacity, per_block, samples)
    arrived, arrived_meta = (
        lax.all_to_all(payload, "tile", split_axis=0, concat_axis=0, tiled=True),
        lax.all_to_all(metadata, "tile", split_axis=0, concat_axis=0, tiled=True),
    )
    received = triangle(arrived.reshape(slots, per_block, samples))
    nodes_in = arrived_meta.reshape(slots, per_block + 1)
    live_flag = (nodes_in[:, 0] > 0.5).astype(jnp.int32)
    live = live_flag.astype(jnp.float32)
    sources = jnp.maximum(nodes_in[:, 0] - 1.0, 0.0).astype(jnp.int32)
    receivers = jnp.maximum(nodes_in[:, 1:] - 1.0, 0.0).astype(jnp.int32)
    time_rows = time_table[:, 0, :]
    amp_rows = amp_table[:, 0, :]
    width_rows = width_table[:, 0, :]
    points = time_rows.shape[1]
    group = math.gcd(slots, max(1, 128 // per_block))
    order = jnp.arange(slots, dtype=jnp.int32)
    rounds = slots // group

    def accumulate(index, total):
        chosen = lax.dynamic_slice_in_dim(order, index * group, group)
        return total + spread(
            jnp.take(received, chosen, axis=0),
            jnp.take(sources, chosen),
            jnp.take(receivers, chosen, axis=0),
            jnp.take(live, chosen),
            time_rows,
            amp_rows,
            width_rows,
        )

    image = lax.fori_loop(0, rounds, accumulate, jnp.zeros((points,), jnp.float32))
    planes = image.reshape(DEPTH, 1, CELLS)
    slab = lax.all_to_all(planes, "offs", split_axis=0, concat_axis=1, tiled=True)
    return slab[None]


def solution(mesh):
    return jax.shard_map(
        body,
        mesh=mesh,
        in_specs=(
            P("offs", "tile", None, None),
            P("offs", "tile"),
            P("offs", "tile", None),
            P("offs", "tile", None),
            P(None, "tile", None),
            P(None, "tile", None),
            P(None, "tile", None),
        ),
        out_specs=P("tile", "offs", None, None),
        check_vma=False,
    )
```

profile of v0, /device:TPU:0, one launch (start us, length us, event | category | flops | bytes accessed | tf_op | source)
XLA Modules:
  0.0 853.8 jit_solution(3695333379503200237)
XLA Ops:
  0.0 0.8 copy.27
  1.4 0.8 fusion.20
  3.0 6.3 all-to-all-start
  9.5 1.1 reshape_squeeze.7
  10.7 1.2 copy_bitcast_fusion
  12.5 1.1 copy.33
  13.6 1.4 all-to-all-done
  14.9 3.7 all-to-all-start.1
  18.9 12.4 %all-to-all-done.1 = f32[8,3,2,2000]{3,2,1,0:T(2,128)S(1)} async-done(((f32[8,3,2,2000]{3,2,1,0:T(2,128)}), f32[8,3,2,2000]{3,2,1,0:T(2,128)S(1)}, u32[]{:S(2)}, u32[]{:S(2)}) %all-to-all-start.1) | async-done | bytes 384032 | tf_op jit(solution)/shard_map/all_to_all | solution.py:79
  31.2 5.9 add_bitcast_fusion.2
  37.8 0.9 copy.35
  38.7 806.3 %while.14 = (s32[]{:T(128)}, f32[2048]{0:T(1024)S(1)}, s32[24]{0:T(128)S(1)}, s32[24]{0:T(128)S(1)}, f32[32,2048]{1,0:T(8,128)S(1)}, /*index=5*/s32[24,2]{1,0:T(...) while((s32[]{:T(128)}, f32[2048]{0:T(1024)S(1)}, ...), condition=%wide.region_4.7_spmd.clone, body=%wide.region_2.6_spmd.clone.sunk | while | flops 1003607 | bytes 16486697 | solution.py:108
  38.8 1.0 copy-done
  39.8 0.9 gather_fusion
  43.5 0.6 gather_fusion.4
  45.8 259.0 %gather_fusion.7 = f32[32768]{0:T(1024)S(1)} fusion(f32[16,6000]{1,0:T(8,128)S(1)} %broadcast_select_fusion.9, s32[32768]{0:T(1024)S(1)} %bitcast.57), kind=kCustom, calls=%fused_computation.10.clone.clone.1 | custom fusion | bytes 524288 | tf_op jit(solution)/shard_map/while/body/eval_jaxpr/jit(take_along_axis)/gather | solution.py:45
  305.8 0.6 gather_fusion.9
  307.5 1.0 copy-done
  308.6 0.9 gather_fusion
  314.6 259.0 %gather_fusion.7 = f32[32768]{0:T(1024)S(1)} fusion(f32[16,6000]{1,0:T(8,128)S(1)} %broadcast_select_fusion.9, s32[32768]{0:T(1024)S(1)} %bitcast.57), kind=kCustom, calls=%fused_computation.10.clone.clone.1 | custom fusion | bytes 524288 | tf_op jit(solution)/shard_map/while/body/eval_jaxpr/jit(take_along_axis)/gather | solution.py:45
  576.3 1.0 copy-done
  577.4 0.9 gather_fusion
  583.4 259.0 %gather_fusion.7 = f32[32768]{0:T(1024)S(1)} fusion(f32[16,6000]{1,0:T(8,128)S(1)} %broadcast_select_fusion.9, s32[32768]{0:T(1024)S(1)} %bitcast.57), kind=kCustom, calls=%fused_computation.10.clone.clone.1 | custom fusion | bytes 524288 | tf_op jit(solution)/shard_map/while/body/eval_jaxpr/jit(take_along_axis)/gather | solution.py:45
  845.0 8.2 all_to_all.25
  (146 shorter events, 25.5 us)
Async XLA Ops:
  0.0 12.4 %copy-start.2 = (f32[32,1,2048]{2,1,0:T(1,128)S(1)}, f32[32,1,2048]{2,1,0:T(1,128)}, u32[]{:S(2)}) copy-start(f32[32,1,2048]{2,1,0:T(1,128)} %param.18) | copy-start | bytes 786436
  3.0 12.0 %all-to-all-start = ((f32[8,3,3]{1,2,0:T(4,128)}), f32[8,3,3]{1,2,0:T(4,128)S(1)}, u32[]{:S(2)}, u32[]{:S(2)}) async-start(f32[8,3,3]{1,2,0:T(4,128)} %copy.28), calls=%async_computation | async-start | bytes 32768 | tf_op jit(solution)/shard_map/all_to_all | solution.py:80
  14.9 16.3 %all-to-all-start.1 = ((f32[8,3,2,2000]{3,2,1,0:T(2,128)}), f32[8,3,2,2000]{3,2,1,0:T(2,128)S(1)}, u32[]{:S(2)}, u32[]{:S(2)}) async-start(f32[8,3,2,2000]{3,2,1,0:T(2,128)} %copy.33), calls=%async_computation.1 | async-start | bytes 786432 | tf_op jit(solution)/shard_map/all_to_all | solution.py:79
  38.7 1.2 copy-start
  305.1 2.3 copy-start.1
  307.4 1.2 copy-start
  573.9 2.3 copy-start.1
  576.2 1.2 copy-start
  842.7 2.3 copy-start.1
where the time goes:
time: 854 us
  local copies, waits for them, and re-layouts  810 us (95%)
  waiting for transfers between devices  13.7 us (2%)
  starting transfers between devices  10.1 us (1%)
  other arithmetic  9.87 us (1%)
    gather x6, local copies, waits for them, and re-layouts, spread(): picked = jnp.take_along_axis(flat, column, axis=1)  777 us
  transfers between devices with their start and end apart: 2, of which 2 were waited for; matrix products, arithmetic and copies ran while one was open for 1% of the time, Pallas kernels for 0%

commit v1 on v0

v1 whole, which is shorter than its diff:
```python
import functools

import jax
import jax.numpy as jnp
from jax import lax
from jax.experimental import pallas as pl
from jax.experimental.pallas import tpu as pltpu
from jax.sharding import PartitionSpec as P

LANES = 128
SUBLANES = 8
VMEM = pl.BlockSpec(memory_space=pltpu.VMEM)
SMEM = pl.BlockSpec(memory_space=pltpu.SMEM)
PARAMS = pltpu.CompilerParams(vmem_limit_bytes=24 << 20)


def pack_kernel(chips, capacity, src, rec, ap, traces, *rest):
    outs, block_of, count = rest[:-2], rest[-2], rest[-1]
    blocks, per_block, samples = traces.shape[1:]
    listed = ap.shape[0]
    me = lax.axis_index("tile")
    z, core = me >> 1, me & 1
    for n in range(2 * chips):
        count[n] = 0
    for n in range(2 * chips * capacity):
        block_of[n] = -1
    for b in range(blocks):
        for e in range(listed):
            tile = ap[e, b]
            group = ((tile >> 1) ^ z) * 2 + ((tile & 1) ^ core)
            place = count[group]
            count[group] = place + 1
            block_of[group * capacity + place] = b
    full, tail = samples // LANES, samples % LANES
    lane = lax.broadcasted_iota(jnp.int32, (per_block, LANES), 1)
    for k in range(chips):
        for slot in range(2 * capacity):
            b = block_of[k * 2 * capacity + slot]
            live = b >= 0
            b = jnp.maximum(b, 0)
            for h in range(full):
                outs[k][slot, per_block * h:per_block * (h + 1), :] = traces[0, b, :, h * LANES:(h + 1) * LANES]
            notes = jnp.where(lane == tail, jnp.where(live, src[0, b] + 1, 0), 0)
            for i in range(per_block):
                notes = jnp.where(lane == tail + 1 + i, rec[i, b], notes)
            outs[k][slot, per_block * full:per_block * (full + 1), :] = notes.astype(jnp.float32)
            outs[k][slot, per_block * full:per_block * (full + 1), 0:tail] = traces[0, b, :, full * LANES:]


def pack(src, rec, ap, traces, chips, capacity):
    rows = traces.shape[2] * -(-traces.shape[3] // LANES)
    return pl.pallas_call(
        functools.partial(pack_kernel, chips, capacity),
        out_shape=[jax.ShapeDtypeStruct((2 * capacity, rows, LANES), jnp.float32)] * chips,
        in_specs=[SMEM, SMEM, SMEM, VMEM],
        out_specs=[VMEM] * chips,
        scratch_shapes=[pltpu.SMEM((2 * chips * capacity,), jnp.int32), pltpu.SMEM((2 * chips,), jnp.int32)],
        compiler_params=PARAMS,
    )(src, rec, ap, traces)


def triangles(x, lane, per_block):
    zero = jnp.zeros((per_block, LANES), jnp.float32)
    after = jnp.concatenate([x[per_block:], zero], 0)
    before = jnp.concatenate([zero, x[:-per_block]], 0)
    pairs = []
    for k in (1, 2, 3, 4):
        ahead = pltpu.roll(jnp.where(lane < k, after, x), LANES - k, 1)
        behind = pltpu.roll(jnp.where(lane >= LANES - k, before, x), k, 1)
        pairs.append(ahead + behind)
    a, b, c, d = pairs
    return (
        0.5 * x + 0.25 * a,
        (3.0 * x + 2.0 * a + b) * (1.0 / 9.0),
        (5.0 * x + 4.0 * a + 3.0 * b + 2.0 * c + d) * (1.0 / 25.0),
    )


def migrate_kernel(capacity, per_block, samples, arrived, t0, a0, w0, t1, a1, w1, image_in, image, filtered, notes, sem):
    rows = arrived.shape[1]
    note_rows = pl.ds(rows - SUBLANES, SUBLANES)
    copy = pltpu.make_async_copy(arrived.at[:, note_rows, :], notes, sem)
    copy.start()
    lane = lax.broadcasted_iota(jnp.int32, (rows, LANES), 1)
    row = lax.broadcasted_iota(jnp.int32, (rows, LANES), 0)
    full, tail = samples // LANES, samples % LANES
    inside = (row < per_block * full) | (lane < tail)
    steps = rows // per_block
    for slot in range(2 * capacity):
        layers = triangles(jnp.where(inside, arrived[slot], 0.0), lane, per_block)
        for c in range(3):
            filtered[slot, c] = layers[c]
    copy.wait()
    note_row = SUBLANES - per_block
    image[...] = image_in[...]

    for q, (times, amps, widths) in enumerate(((t0, a0, w0), (t1, a1, w1))):
        live = jnp.int32(0)
        for j in range(capacity):
            live = live + (notes[q * capacity + j, note_row, tail] > 0.5).astype(jnp.int32)

        def add_slot(j, _, q=q, times=times, amps=amps, widths=widths):
            slot = q * capacity + j
            s = notes[slot, note_row, tail].astype(jnp.int32) - 1
            for i in range(per_block):
                r = notes[slot, note_row, tail + 1 + i].astype(jnp.int32)
                for half in range(times.shape[1] // SUBLANES):
                    part = pl.ds(SUBLANES * half, SUBLANES)
                    t = times[s, part] + times[r, part]
                    c = jnp.maximum(widths[s, part], widths[r, part])
                    weight = amps[s, part] * amps[r, part]
                    within = t & (LANES - 1)
                    wanted = c * steps + (t >> 7)
                    total = None
                    for c in range(3):
                        for h in range(steps):
                            line = filtered[slot, c, pl.ds(per_block * h + i, 1), :]
                            got = jnp.take_along_axis(
                                jnp.broadcast_to(line, (SUBLANES, LANES)), within, axis=1
                            )
                            total = got if total is None else jnp.where(wanted == c * steps + h, got, total)
                    image[q, part] += weight * total
            return 0

        lax.fori_loop(0, live, add_slot, 0)


def migrate(arrived, own, sibling, image, per_block, samples):
    capacity = arrived.shape[0] // 2
    return pl.pallas_call(
        functools.partial(migrate_kernel, capacity, per_block, samples),
        out_shape=jax.ShapeDtypeStruct(image.shape, jnp.float32),
        in_specs=[VMEM] * 8,
        out_specs=VMEM,
        scratch_shapes=[
            pltpu.VMEM((2 * capacity, 3) + arrived.shape[1:], jnp.float32),
            pltpu.SMEM((2 * capacity, SUBLANES, LANES), jnp.float32),
            pltpu.SemaphoreType.DMA,
        ],
        compiler_params=PARAMS,
        cost_estimate=pl.CostEstimate(flops=20_000_000, bytes_accessed=2_000_000, transcendentals=0),
    )(arrived, *own, *sibling, image)


def slab_kernel(classes, mine, other, *outs):
    me = lax.axis_index("offs")
    depth = outs[0].shape[0]
    whole = mine[0] + other[...]
    image = outs[-1]
    image[...] = whole
    for k in range(classes):
        outs[k][...] = image[pl.ds((me ^ k) * depth, depth), :]


def slabs(mine, other, classes):
    shape = other.shape
    part = jax.ShapeDtypeStruct((shape[0] // classes, shape[1]), jnp.float32)
    return pl.pallas_call(
        functools.partial(slab_kernel, classes),
        out_shape=[part] * classes,
        in_specs=[VMEM] * 2,
        out_specs=[VMEM] * classes,
        scratch_shapes=[pltpu.VMEM(shape, jnp.float32)],
        compiler_params=PARAMS,
    )(mine, other)


def gather_kernel(classes, *refs):
    out = refs[-1]
    me = lax.axis_index("offs")
    depth = out.shape[1]
    for k in range(classes):
        for d in range(depth):
            out[0, d, pl.ds(me ^ k, 1), :] = refs[k][pl.ds(d, 1), :]


def assemble(parts):
    classes = len(parts)
    depth, cells = parts[0].shape
    return pl.pallas_call(
        functools.partial(gather_kernel, classes),
        out_shape=jax.ShapeDtypeStruct((1, depth, classes, cells), jnp.float32),
        in_specs=[VMEM] * classes,
        out_specs=VMEM,
        compiler_params=PARAMS,
    )(*parts)


def swap(value, axis, k):
    size = lax.axis_size(axis)
    return lax.ppermute(value, axis, [(i, i ^ k) for i in range(size)])


def body(traces, src_node, rec_node, aperture, time_table, amp_table, width_table):
    tiles = lax.axis_size("tile")
    classes = lax.axis_size("offs")
    chips = tiles // 2
    blocks, per_block, samples = traces.shape[1:]
    listed = aperture.shape[2]
    capacity = (3 * blocks * listed + 2 * tiles - 1) // (2 * tiles)
    nodes, _, points = time_table.shape
    own = tuple(t.reshape(nodes, points // LANES, LANES) for t in (time_table, amp_table, width_table))

    packed = pack(src_node, rec_node[0].T, aperture[0].T, traces, chips, capacity)
    arrived = [packed[0]] + [swap(packed[k], "tile", 2 * k) for k in range(1, chips)]
    sibling = tuple(swap(t, "tile", 1) for t in own)
    image = jnp.zeros((2, points // LANES, LANES), jnp.float32)
    for k in range(chips):
        image = migrate(arrived[k], own, sibling, image, per_block, samples)
    parts = slabs(image, swap(image[1], "tile", 1), classes)
    return assemble([parts[0]] + [swap(parts[k], "offs", k) for k in range(1, classes)])


def solution(mesh):
    return jax.shard_map(
        body,
        mesh=mesh,
        in_specs=(
            P("offs", "tile", None, None),
            P("offs", "tile"),
            P("offs", "tile", None),
            P("offs", "tile", None),
            P(None, "tile", None),
            P(None, "tile", None),
            P(None, "tile", None),
        ),
        out_specs=P("tile", "offs", None, None),
        check_vma=False,
    )
```

time: 854 us -> 31.5 us (0.04)
  local copies, waits for them, and re-layouts: 810 us -> 4.46 us
  Pallas kernels: 0 us -> 12 us
  other arithmetic: 9.87 us -> 0 us
    gather x51 -> x0, local copies, waits for them, and re-layouts: 798 us -> none  [the longest x6 777 us: spread(): picked = jnp.take_along_axis(flat, column, axis=1)]
    all_to_all x2 -> x0, waiting for transfers between devices: 13.7 us -> none  [the longest x1 12.4 us: body(): lax.all_to_all(payload, 'tile', split_axis=0, concat_axis=0, tiled=True)]
    pallas_call x0 -> x7, Pallas kernels: none -> 12 us  [the longest x4 10.6 us: migrate(): pl.pallas_call(functools.partial(migrate_kernel, capacity, per_block, sam...]
    all_to_all x2 -> x0, starting transfers between devices: 10.1 us -> none  [the longest x1 6.33 us: body(): lax.all_to_all(metadata, 'tile', split_axis=0, concat_axis=0, tiled=True)]
    ppermute x0 -> x10, starting transfers between devices: none -> 9.75 us  [swap(): return lax.ppermute(value, axis, [(i, i ^ k) for i in range(size)])]
  transfers between devices with their start and end apart: 2 -> 10, of which waited for: 2 -> 4; matrix products, arithmetic and copies ran while one was open for 1% -> 0% of each run, Pallas kernels for 0% -> 27%
where the time goes in v1:
time: 31.5 us; the launch traced here: 31.7 us
  Pallas kernels  12 us (38%)
  starting transfers between devices  9.75 us (31%)
  waiting for transfers between devices  5.38 us (17%)
  local copies, waits for them, and re-layouts  4.46 us (14%)
    pallas_call x4, Pallas kernels, migrate(): pl.pallas_call(functools.partial(migrate_kernel, capacity, per_block, sam...  10.6 us
    ppermute x10, starting transfers between devices, swap(): return lax.ppermute(value, axis, [(i, i ^ k) for i in range(size)])  9.75 us
    ppermute x10, waiting for transfers between devices, swap(): return lax.ppermute(value, axis, [(i, i ^ k) for i in range(size)])  5.38 us
    unnamed x20, local copies, waits for them, and re-layouts  4.45 us
    pallas_call x1, Pallas kernels, pack(): pl.pallas_call(functools.partial(pack_kernel, chips, capacity), out_shape...  0.78 us
  transfers between devices with their start and end apart: 10, of which 4 were waited for; matrix products, arithmetic and copies ran while one was open for 0% of the time, Pallas kernels for 27%

profile of v1, /device:TPU:0, one launch (start us, length us, event | category | flops | bytes accessed | tf_op | source)
XLA Modules:
  0.0 31.7 jit_solution(13668241847710327065)
XLA Ops:
  0.0 0.5 %collective-permute-start.1 = (s32[32,16,128]{2,1,0:T(8,128)}, s32[32,16,128]{2,1,0:T(8,128)S(1)}, u32[]{:S(2)}, u32[]{:S(2)}) collective-permute-start(s32[32,16,128]{2,1,0:T(8,128)} %bitcast.11), channel_id=1, source_target_pairs={{0,4},{4,0},{8,12},{12,8},{16,20},{20,16},{24,28},{28,24},{1,5},{5... | collective-permute-start | bytes 786440 | tf_op jit(solution)/shard_map/ppermute | solution.py:191
  0.5 0.1 collective-permute-start.2
  0.5 0.5 %collective-permute-start.3 = (s32[32,16,128]{2,1,0:T(8,128)}, s32[32,16,128]{2,1,0:T(8,128)S(1)}, u32[]{:S(2)}, u32[]{:S(2)}) collective-permute-start(s32[32,16,128]{2,1,0:T(8,128)} %bitcast.21), channel_id=1, source_target_pairs={{0,4},{4,0},{8,12},{12,8},{16,20},{20,16},{24,28},{28,24},{1,5},{5... | collective-permute-start | bytes 786440 | tf_op jit(solution)/shard_map/ppermute | solution.py:191
  1.0 0.7 %copy-done.8 = s32[1,8,2]{1,2,0:T(2,128)S(1)} copy-done((s32[1,8,2]{1,2,0:T(2,128)S(1)}, s32[1,8,2]{1,2,0:T(2,128)}, u32[]{:S(2)}) %copy-start.8) | copy-done | bytes 88
  1.7 0.9 %copy-done.6 = f32[1,8,2,2000]{3,2,1,0:T(2,128)S(1)} copy-done((f32[1,8,2,2000]{3,2,1,0:T(2,128)S(1)}, f32[1,8,2,2000]{3,2,1,0:T(2,128)}, u32[]{:S(2)}) %copy-start.6) | copy-done | bytes 128024
  2.6 0.8 %shard_map.73 = (f32[6,32,128]{2,1,0:T(8,128)S(1)}, f32[6,32,128]{2,1,0:T(8,128)S(1)}, f32[6,32,128]{2,1,0:T(8,128)S(1)}, f32[6,32,128]{2,1,0:T(8,128)S(1)}) custom-call(s32[1,8]{1,0:T(1,128)S(1)} %copy-done.9, s32[2,8]{1,0:T(2,128)S(1)} %bitcast.26, s32[2,8]{1,0:T(2,128)S(1)} %bitcast.27, f32[1,8,2,2000]{3,2,1,0:T(2,128)S(1)} %copy-done.6), custom_call_target="tpu_custom_call" | custom-call | tf_op jit(solution)/shard_map/pallas_call | solution.py:52
  3.4 2.6 %collective-permute-start.5 = (f32[6,32,128]{2,1,0:T(8,128)S(1)}, f32[6,32,128]{2,1,0:T(8,128)S(1)}, u32[]{:S(2)}, u32[]{:S(2)}) collective-permute-start(f32[6,32,128]{2,1,0:T(8,128)S(1)} %get-tuple-element.15), channel_id=1, source_target_pairs={{0,8},{4,12},{8,0},{12,4},{16,24},{20,28},{24,16},{28,20},{1,9},{5... | collective-permute-start | bytes 294920 | tf_op jit(solution)/shard_map/ppermute | solution.py:191
  6.0 2.6 %collective-permute-start.4 = (f32[6,32,128]{2,1,0:T(8,128)S(1)}, f32[6,32,128]{2,1,0:T(8,128)S(1)}, u32[]{:S(2)}, u32[]{:S(2)}) collective-permute-start(f32[6,32,128]{2,1,0:T(8,128)S(1)} %get-tuple-element.14), channel_id=1, source_target_pairs={{0,16},{4,20},{8,24},{12,28},{16,0},{20,4},{24,8},{28,12},{1,17},{... | collective-permute-start | bytes 294920 | tf_op jit(solution)/shard_map/ppermute | solution.py:191
  8.6 0.9 %copy-done = s32[32,1,2048]{2,1,0:T(1,128)S(1)} copy-done((s32[32,1,2048]{2,1,0:T(1,128)S(1)}, s32[32,1,2048]{2,1,0:T(1,128)}, u32[]{:S(2)}) %copy-start) | copy-done | bytes 262168
  9.6 0.9 %copy-done.2 = f32[32,1,2048]{2,1,0:T(1,128)S(1)} copy-done((f32[32,1,2048]{2,1,0:T(1,128)S(1)}, f32[32,1,2048]{2,1,0:T(1,128)}, u32[]{:S(2)}) %copy-start.2) | copy-done | bytes 262168
  10.5 0.9 %copy-done.4 = s32[32,1,2048]{2,1,0:T(1,128)S(1)} copy-done((s32[32,1,2048]{2,1,0:T(1,128)S(1)}, s32[32,1,2048]{2,1,0:T(1,128)}, u32[]{:S(2)}) %copy-start.4) | copy-done | bytes 262168
  11.5 2.6 %shard_map.74.image_in = f32[2,16,128]{2,1,0:T(8,128)S(1)} custom-call(f32[6,32,128]{2,1,0:T(8,128)S(1)} %get-tuple-element.16.arrived, s32[32,16,128]{2,1,0:T(8,128)S(1)} %bitcast.12, f32[32,16,128]{2,1,0:T(8,128)S(1)} %bitcast.17, s32[32,16,128]{2,1,0:T(8,128)S(1)} %bitcast.22, s32[32,16,128]{2,1,0:T(8,128)S(1)} %collective-permute-done.1.t1, ...), custom_call_target="tpu_custom_call" | custom-call | flops 20000000 | bytes 2000000 | tf_op jit(solution)/shard_map/pallas_call | solution.py:130
  14.2 2.6 %shard_map.75.image_in = f32[2,16,128]{2,1,0:T(8,128)S(1)} custom-call(f32[6,32,128]{2,1,0:T(8,128)S(1)} %collective-permute-done.5.arrived, s32[32,16,128]{2,1,0:T(8,128)S(1)} %bitcast.13, f32[32,16,128]{2,1,0:T(8,128)S(1)} %bitcast.18, s32[32,16,128]{2,1,0:T(8,128)S(1)} %bitcast.23, s32[32,16,128]{2,1,0:T(8,128)S(1)} %collective-permute-done.1.t1, ...), custom_call_target="tpu_custom_call" | custom-call | flops 20000000 | bytes 2000000 | tf_op jit(solution)/shard_map/pallas_call | solution.py:130
  16.8 2.6 %shard_map.76.image_in = f32[2,16,128]{2,1,0:T(8,128)S(1)} custom-call(f32[6,32,128]{2,1,0:T(8,128)S(1)} %collective-permute-done.4.arrived, s32[32,16,128]{2,1,0:T(8,128)S(1)} %bitcast.14, f32[32,16,128]{2,1,0:T(8,128)S(1)} %bitcast.19, s32[32,16,128]{2,1,0:T(8,128)S(1)} %bitcast.24, s32[32,16,128]{2,1,0:T(8,128)S(1)} %collective-permute-done.1.t1, ...), custom_call_target="tpu_custom_call" | custom-call | flops 20000000 | bytes 2000000 | tf_op jit(solution)/shard_map/pallas_call | solution.py:130
  19.5 2.6 %shard_map.77.mine = f32[2,16,128]{2,1,0:T(8,128)S(1)} custom-call(f32[6,32,128]{2,1,0:T(8,128)S(1)} %collective-permute-done.arrived, s32[32,16,128]{2,1,0:T(8,128)S(1)} %bitcast.15, f32[32,16,128]{2,1,0:T(8,128)S(1)} %bitcast.20, s32[32,16,128]{2,1,0:T(8,128)S(1)} %bitcast.25, s32[32,16,128]{2,1,0:T(8,128)S(1)} %collective-permute-done.1.t1, ...), custom_call_target="tpu_custom_call" | custom-call | flops 20000000 | bytes 2000000 | tf_op jit(solution)/shard_map/pallas_call | solution.py:130
  22.1 0.1 collective-permute-start.6
  22.2 1.2 %collective-permute-done.6.other = f32[16,128]{1,0:T(8,128)S(1)} collective-permute-done((f32[16,128]{1,0:T(8,128)S(1)}, f32[16,128]{1,0:T(8,128)S(1)}, u32[]{:S(2)}, u32[]{:S(2)}) %collective-permute-start.6) | collective-permute-done | bytes 8224 | tf_op jit(solution)/shard_map/ppermute | solution.py:191
  23.4 1.7 %collective-permute-start.7 = (f32[4,128]{1,0:T(4,128)S(1)}, f32[4,128]{1,0:T(4,128)S(1)}, u32[]{:S(2)}, u32[]{:S(2)}) collective-permute-start(f32[4,128]{1,0:T(4,128)S(1)} %get-tuple-element.18), channel_id=1, source_target_pairs={{0,1},{1,0},{2,3},{3,2},{4,5},{5,4},{6,7},{7,6},{8,9},{9,8},{10,11... | collective-permute-start | bytes 6152 | tf_op jit(solution)/shard_map/ppermute | solution.py:191
  25.1 1.5 %collective-permute-start.8 = (f32[4,128]{1,0:T(4,128)S(1)}, f32[4,128]{1,0:T(4,128)S(1)}, u32[]{:S(2)}, u32[]{:S(2)}) collective-permute-start(f32[4,128]{1,0:T(4,128)S(1)} %get-tuple-element.19), channel_id=1, source_target_pairs={{0,2},{1,3},{2,0},{3,1},{4,6},{5,7},{6,4},{7,5},{8,10},{9,11},{10,... | collective-permute-start | bytes 6152 | tf_op jit(solution)/shard_map/ppermute | solution.py:191
  26.6 0.3 collective-permute-start.9
  26.9 0.1 collective-permute-done.7.refs_1_
  27.0 1.7 %collective-permute-done.8.refs_2_ = f32[4,128]{1,0:T(4,128)S(1)} collective-permute-done((f32[4,128]{1,0:T(4,128)S(1)}, f32[4,128]{1,0:T(4,128)S(1)}, u32[]{:S(2)}, u32[]{:S(2)}) %collective-permute-start.8) | collective-permute-done | bytes 2080 | tf_op jit(solution)/shard_map/ppermute | solution.py:191
  28.7 2.4 %collective-permute-done.9.refs_3_ = f32[4,128]{1,0:T(4,128)S(1)} collective-permute-done((f32[4,128]{1,0:T(4,128)S(1)}, f32[4,128]{1,0:T(4,128)S(1)}, u32[]{:S(2)}, u32[]{:S(2)}) %collective-permute-start.9) | collective-permute-done | bytes 2080 | tf_op jit(solution)/shard_map/ppermute | solution.py:191
  31.1 0.6 %shard_map.79 = f32[1,4,4,128]{3,2,1,0:T(4,128)} custom-call(f32[4,128]{1,0:T(4,128)S(1)} %get-tuple-element.17.refs_0_, f32[4,128]{1,0:T(4,128)S(1)} %collective-permute-done.7.refs_1_, f32[4,128]{1,0:T(4,128)S(1)} %collective-permute-done.8.refs_2_, f32[4,128]{1,0:T(4,128)S(1)} %collective-permute-done.9.refs_3_), custom_call_target="tpu_custom_call" | custom-call | tf_op jit(solution)/shard_map/pallas_call | solution.py:180
  (25 shorter events, 0.1 us)
Async XLA Ops:
  0.0 8.6 %collective-permute-start.1 = (s32[32,16,128]{2,1,0:T(8,128)}, s32[32,16,128]{2,1,0:T(8,128)S(1)}, u32[]{:S(2)}, u32[]{:S(2)}) collective-permute-start(s32[32,16,128]{2,1,0:T(8,128)} %bitcast.11), channel_id=1, source_target_pairs={{0,4},{4,0},{8,12},{12,8},{16,20},{20,16},{24,28},{28,24},{1,5},{5... | collective-permute-start | bytes 786440 | tf_op jit(solution)/shard_map/ppermute | solution.py:191
  0.5 8.1 %collective-permute-start.2 = (f32[32,16,128]{2,1,0:T(8,128)}, f32[32,16,128]{2,1,0:T(8,128)S(1)}, u32[]{:S(2)}, u32[]{:S(2)}) collective-permute-start(f32[32,16,128]{2,1,0:T(8,128)} %bitcast.16), channel_id=1, source_target_pairs={{0,4},{4,0},{8,12},{12,8},{16,20},{20,16},{24,28},{28,24},{1,5},{5... | collective-permute-start | bytes 786440 | tf_op jit(solution)/shard_map/ppermute | solution.py:191
  0.5 8.1 %collective-permute-start.3 = (s32[32,16,128]{2,1,0:T(8,128)}, s32[32,16,128]{2,1,0:T(8,128)S(1)}, u32[]{:S(2)}, u32[]{:S(2)}) collective-permute-start(s32[32,16,128]{2,1,0:T(8,128)} %bitcast.21), channel_id=1, source_target_pairs={{0,4},{4,0},{8,12},{12,8},{16,20},{20,16},{24,28},{28,24},{1,5},{5... | collective-permute-start | bytes 786440 | tf_op jit(solution)/shard_map/ppermute | solution.py:191
  1.0 0.7 %copy-start.8 = (s32[1,8,2]{1,2,0:T(2,128)S(1)}, s32[1,8,2]{1,2,0:T(2,128)}, u32[]{:S(2)}) copy-start(s32[1,8,2]{1,2,0:T(2,128)} %param.10) | copy-start | bytes 196
  1.0 0.7 %copy-start.7 = (s32[1,8,2]{1,2,0:T(2,128)S(1)}, s32[1,8,2]{1,2,0:T(2,128)}, u32[]{:S(2)}) copy-start(s32[1,8,2]{1,2,0:T(2,128)} %param.9) | copy-start | bytes 196
  1.0 0.7 %copy-start.9 = (s32[1,8]{1,0:T(1,128)S(1)}, s32[1,8]{1,0:T(1,128)}, u32[]{:S(2)}) copy-start(s32[1,8]{1,0:T(1,128)} %src.1) | copy-start | bytes 100
  1.7 0.9 %copy-start.6 = (f32[1,8,2,2000]{3,2,1,0:T(2,128)S(1)}, f32[1,8,2,2000]{3,2,1,0:T(2,128)}, u32[]{:S(2)}) copy-start(f32[1,8,2,2000]{3,2,1,0:T(2,128)} %traces.1) | copy-start | bytes 384004
  3.4 10.8 %collective-permute-start.5 = (f32[6,32,128]{2,1,0:T(8,128)S(1)}, f32[6,32,128]{2,1,0:T(8,128)S(1)}, u32[]{:S(2)}, u32[]{:S(2)}) collective-permute-start(f32[6,32,128]{2,1,0:T(8,128)S(1)} %get-tuple-element.15), channel_id=1, source_target_pairs={{0,8},{4,12},{8,0},{12,4},{16,24},{20,28},{24,16},{28,20},{1,9},{5... | collective-permute-start | bytes 294920 | tf_op jit(solution)/shard_map/ppermute | solution.py:191
  6.0 10.8 %collective-permute-start.4 = (f32[6,32,128]{2,1,0:T(8,128)S(1)}, f32[6,32,128]{2,1,0:T(8,128)S(1)}, u32[]{:S(2)}, u32[]{:S(2)}) collective-permute-start(f32[6,32,128]{2,1,0:T(8,128)S(1)} %get-tuple-element.14), channel_id=1, source_target_pairs={{0,16},{4,20},{8,24},{12,28},{16,0},{20,4},{24,8},{28,12},{1,17},{... | collective-permute-start | bytes 294920 | tf_op jit(solution)/shard_map/ppermute | solution.py:191
  8.6 10.9 %collective-permute-start = (f32[6,32,128]{2,1,0:T(8,128)S(1)}, f32[6,32,128]{2,1,0:T(8,128)S(1)}, u32[]{:S(2)}, u32[]{:S(2)}) collective-permute-start(f32[6,32,128]{2,1,0:T(8,128)S(1)} %get-tuple-element.13), channel_id=1, source_target_pairs={{0,24},{4,28},{8,16},{12,20},{16,8},{20,12},{24,0},{28,4},{1,25},{... | collective-permute-start | bytes 294920 | tf_op jit(solution)/shard_map/ppermute | solution.py:191
  8.6 1.0 %copy-start = (s32[32,1,2048]{2,1,0:T(1,128)S(1)}, s32[32,1,2048]{2,1,0:T(1,128)}, u32[]{:S(2)}) copy-start(s32[32,1,2048]{2,1,0:T(1,128)} %param.11) | copy-start | bytes 786436
  9.6 0.9 %copy-start.2 = (f32[32,1,2048]{2,1,0:T(1,128)S(1)}, f32[32,1,2048]{2,1,0:T(1,128)}, u32[]{:S(2)}) copy-start(f32[32,1,2048]{2,1,0:T(1,128)} %param.12) | copy-start | bytes 786436
  10.5 0.9 %copy-start.4 = (s32[32,1,2048]{2,1,0:T(1,128)S(1)}, s32[32,1,2048]{2,1,0:T(1,128)}, u32[]{:S(2)}) copy-start(s32[32,1,2048]{2,1,0:T(1,128)} %param.13) | copy-start | bytes 786436
  11.5 2.7 %copy-start.1 = (s32[32,1,2048]{2,1,0:T(1,128)S(1)}, s32[32,1,2048]{2,1,0:T(1,128)}, u32[]{:S(2)}) copy-start(s32[32,1,2048]{2,1,0:T(1,128)} %param.11) | copy-start | bytes 786436
  11.5 2.7 %copy-start.3 = (f32[32,1,2048]{2,1,0:T(1,128)S(1)}, f32[32,1,2048]{2,1,0:T(1,128)}, u32[]{:S(2)}) copy-start(f32[32,1,2048]{2,1,0:T(1,128)} %param.12) | copy-start | bytes 786436
  11.5 2.7 %copy-start.5 = (s32[32,1,2048]{2,1,0:T(1,128)S(1)}, s32[32,1,2048]{2,1,0:T(1,128)}, u32[]{:S(2)}) copy-start(s32[32,1,2048]{2,1,0:T(1,128)} %param.13) | copy-start | bytes 786436
  22.1 1.2 %collective-permute-start.6 = (f32[16,128]{1,0:T(8,128)S(1)}, f32[16,128]{1,0:T(8,128)S(1)}, u32[]{:S(2)}, u32[]{:S(2)}) collective-permute-start(f32[16,128]{1,0:T(8,128)S(1)} %slice_bitcast_fusion), channel_id=1, source_target_pairs={{0,4},{4,0},{8,12},{12,8},{16,20},{20,16},{24,28},{28,24},{1,5},{5... | collective-permute-start | bytes 24584 | tf_op jit(solution)/shard_map/ppermute | solution.py:191
  23.4 3.6 %collective-permute-start.7 = (f32[4,128]{1,0:T(4,128)S(1)}, f32[4,128]{1,0:T(4,128)S(1)}, u32[]{:S(2)}, u32[]{:S(2)}) collective-permute-start(f32[4,128]{1,0:T(4,128)S(1)} %get-tuple-element.18), channel_id=1, source_target_pairs={{0,1},{1,0},{2,3},{3,2},{4,5},{5,4},{6,7},{7,6},{8,9},{9,8},{10,11... | collective-permute-start | bytes 6152 | tf_op jit(solution)/shard_map/ppermute | solution.py:191
  25.1 3.6 %collective-permute-start.8 = (f32[4,128]{1,0:T(4,128)S(1)}, f32[4,128]{1,0:T(4,128)S(1)}, u32[]{:S(2)}, u32[]{:S(2)}) collective-permute-start(f32[4,128]{1,0:T(4,128)S(1)} %get-tuple-element.19), channel_id=1, source_target_pairs={{0,2},{1,3},{2,0},{3,1},{4,6},{5,7},{6,4},{7,5},{8,10},{9,11},{10,... | collective-permute-start | bytes 6152 | tf_op jit(solution)/shard_map/ppermute | solution.py:191
  26.6 4.5 %collective-permute-start.9 = (f32[4,128]{1,0:T(4,128)S(1)}, f32[4,128]{1,0:T(4,128)S(1)}, u32[]{:S(2)}, u32[]{:S(2)}) collective-permute-start(f32[4,128]{1,0:T(4,128)S(1)} %get-tuple-element.20), channel_id=1, source_target_pairs={{0,3},{1,2},{2,1},{3,0},{4,7},{5,6},{6,5},{7,4},{8,11},{9,10},{10,... | collective-permute-start | bytes 6152 | tf_op jit(solution)/shard_map/ppermute | solution.py:191

commit v2 on v1

v2 whole, which is shorter than its diff:
```python
import functools
import math

import jax
import jax.numpy as jnp
from jax import lax
from jax.experimental import pallas as pl
from jax.experimental.pallas import tpu as pltpu
from jax.sharding import PartitionSpec as P

LANES = 128
SUBLANES = 8
VMEM = pl.BlockSpec(memory_space=pltpu.VMEM)
HBM = pl.BlockSpec(memory_space=pltpu.HBM)
HALF_WIDTHS = (1, 2, 4)
PARAMS = pltpu.CompilerParams(vmem_limit_bytes=24 << 20)


def pack_kernel(chips, capacity, src_in, rec_in, ap_in, traces_in, *rest):
    outs = rest[:chips]
    src, rec, ap, traces, block_of, count, sems = rest[chips:]
    copies = [
        pltpu.make_async_copy(a, b, sems.at[n])
        for n, (a, b) in enumerate(((ap_in, ap), (src_in, src), (rec_in, rec)))
    ]
    blocks, per_block, samples = traces.shape
    pieces = sems.shape[0] - 3
    size = blocks // pieces
    for n in range(pieces):
        part = pl.ds(n * size, size)
        copies.append(pltpu.make_async_copy(traces_in.at[0, part], traces.at[part], sems.at[3 + n]))
    for copy in copies:
        copy.start()
    listed = ap.shape[0]
    me = lax.axis_index("tile")
    z, core = me >> 1, me & 1
    for n in range(2 * chips):
        count[n] = 0
    for n in range(2 * chips * capacity):
        block_of[n] = -1
    copies[0].wait()
    for b in range(blocks):
        for e in range(listed):
            tile = ap[e, b]
            group = ((tile >> 1) ^ z) * 2 + ((tile & 1) ^ core)
            place = count[group]
            count[group] = place + 1
            block_of[group * capacity + place] = b
    for copy in copies[1:]:
        copy.wait()
    full, tail = samples // LANES, samples % LANES
    lane = lax.broadcasted_iota(jnp.int32, (per_block, LANES), 1)
    for k in range(chips):
        for slot in range(2 * capacity):
            b = block_of[k * 2 * capacity + slot]
            live = b >= 0
            b = jnp.maximum(b, 0)
            for h in range(full):
                outs[k][slot, per_block * h:per_block * (h + 1), :] = traces[b, :, h * LANES:(h + 1) * LANES]
            notes = jnp.where(lane == tail, jnp.where(live, src[0, b] + 1, 0), 0)
            for i in range(per_block):
                notes = jnp.where(lane == tail + 1 + i, rec[i, b], notes)
            outs[k][slot, per_block * full:per_block * (full + 1), :] = notes.astype(jnp.float32)
            outs[k][slot, per_block * full:per_block * (full + 1), 0:tail] = traces[b, :, full * LANES:]


def pack(src, rec, ap, traces, chips, capacity):
    blocks, per_block, samples = traces.shape[1:]
    rows = per_block * -(-samples // LANES)
    pieces = math.gcd(blocks, 4)
    return pl.pallas_call(
        functools.partial(pack_kernel, chips, capacity),
        out_shape=[jax.ShapeDtypeStruct((2 * capacity, rows, LANES), jnp.float32)] * chips,
        in_specs=[HBM] * 4,
        out_specs=[VMEM] * chips,
        scratch_shapes=[
            pltpu.SMEM(src.shape, jnp.int32),
            pltpu.SMEM(rec.shape, jnp.int32),
            pltpu.SMEM(ap.shape, jnp.int32),
            pltpu.VMEM(traces.shape[1:], jnp.float32),
            pltpu.SMEM((2 * chips * capacity,), jnp.int32),
            pltpu.SMEM((2 * chips,), jnp.int32),
            pltpu.SemaphoreType.DMA((3 + pieces,)),
        ],
        compiler_params=PARAMS,
    )(src, rec, ap, traces)


def filter_matrix():
    shape = (2 * LANES, LANES)
    row = lax.broadcasted_iota(jnp.int32, shape, 0)
    column = lax.broadcasted_iota(jnp.int32, shape, 1)
    where = jnp.where(row >= LANES + LANES // 2, row - 2 * LANES, row)
    distance = jnp.abs(where - column)
    return [jnp.maximum(h + 1 - distance, 0).astype(jnp.float32).astype(jnp.bfloat16) for h in HALF_WIDTHS]


def filter_slots(arrived, matrix, filtered, per_block, samples):
    slots, rows, _ = arrived.shape
    lane = lax.broadcasted_iota(jnp.int32, (rows, LANES), 1)
    row = lax.broadcasted_iota(jnp.int32, (rows, LANES), 0)
    inside = (row < per_block * (samples // LANES)) | (lane < samples % LANES)
    zero = jnp.zeros((per_block, LANES), jnp.float32)
    for slot in range(slots):
        x = jnp.where(inside, arrived[slot], 0.0)
        after = jnp.concatenate([x[per_block:], zero], 0)
        before = jnp.concatenate([zero, x[:-per_block]], 0)
        wide = jnp.concatenate([x, jnp.where(lane < LANES // 2, after, before)], 1)
        high = wide.astype(jnp.bfloat16)
        rest = wide - high.astype(jnp.float32)
        middle = rest.astype(jnp.bfloat16)
        low = (rest - middle.astype(jnp.float32)).astype(jnp.bfloat16)
        pieces = jnp.concatenate([high, middle, low], 0)
        for c, h in enumerate(HALF_WIDTHS):
            product = jnp.dot(pieces, matrix[c], preferred_element_type=jnp.float32)
            summed = product[:rows] + (product[rows:2 * rows] + product[2 * rows:])
            filtered[slot, c] = summed * (1.0 / (h + 1) ** 2)


def add_slots(q, capacity, notes, filtered, tables, image, per_block, samples):
    times, amps, widths = tables
    note_row = SUBLANES - per_block
    tail = samples % LANES
    steps = filtered.shape[2] // per_block
    live = jnp.int32(0)
    for j in range(capacity):
        live = live + (notes[q * capacity + j, note_row, tail] > 0.5).astype(jnp.int32)

    def add_slot(j, _):
        slot = q * capacity + j
        s = notes[slot, note_row, tail].astype(jnp.int32) - 1
        for i in range(per_block):
            r = notes[slot, note_row, tail + 1 + i].astype(jnp.int32)
            for half in range(times.shape[1] // SUBLANES):
                part = pl.ds(SUBLANES * half, SUBLANES)
                t = times[s, part] + times[r, part]
                c = jnp.maximum(widths[s, part], widths[r, part])
                weight = amps[s, part] * amps[r, part]
                within = t & (LANES - 1)
                wanted = c * steps + (t >> 7)
                total = None
                for c in range(3):
                    for h in range(steps):
                        line = filtered[slot, c, pl.ds(per_block * h + i, 1), :]
                        got = jnp.take_along_axis(jnp.broadcast_to(line, (SUBLANES, LANES)), within, axis=1)
                        total = got if total is None else jnp.where(wanted == c * steps + h, got, total)
                image[q, part] += weight * total
        return 0

    lax.fori_loop(0, live, add_slot, 0)


def note_copy(arrived, notes, sem):
    part = pl.ds(arrived.shape[1] - SUBLANES, SUBLANES)
    return pltpu.make_async_copy(arrived.at[:, part, :], notes, sem)


def first_kernel(
    capacity, per_block, samples, arrived, own0, own1, own2, sib0, sib1, sib2,
    image, times, amps, widths, matrix, filtered, notes, sems,
):
    pairs = ((own0, times), (own1, amps), (own2, widths))
    loads = []
    pieces = (sems.shape[0] - 1) // 3
    size = times.shape[0] // pieces
    for n, (a, b) in enumerate(pairs):
        for m in range(pieces):
            part = pl.ds(m * size, size)
            loads.append(pltpu.make_async_copy(a.at[part], b.at[part], sems.at[1 + n * pieces + m]))
    copy = note_copy(arrived, notes, sems.at[0])
    copy.start()
    for load in loads:
        load.start()
    layers = filter_matrix()
    for c in range(3):
        matrix[c] = layers[c]
    filter_slots(arrived, matrix, filtered, per_block, samples)
    image[...] = jnp.zeros(image.shape, jnp.float32)
    copy.wait()
    add_slots(1, capacity, notes, filtered, (sib0, sib1, sib2), image, per_block, samples)
    for load in loads:
        load.wait()
    add_slots(0, capacity, notes, filtered, (times, amps, widths), image, per_block, samples)


def next_kernel(
    capacity, per_block, samples, arrived, own0, own1, own2, sib0, sib1, sib2, matrix, image_in,
    image, filtered, notes, sem,
):
    copy = note_copy(arrived, notes, sem)
    copy.start()
    filter_slots(arrived, matrix, filtered, per_block, samples)
    image[...] = image_in[...]
    copy.wait()
    add_slots(1, capacity, notes, filtered, (sib0, sib1, sib2), image, per_block, samples)
    add_slots(0, capacity, notes, filtered, (own0, own1, own2), image, per_block, samples)


COST = pl.CostEstimate(flops=20_000_000, bytes_accessed=2_000_000, transcendentals=0)


def migrate_scratch(arrived):
    slots = arrived.shape[0]
    return [
        pltpu.VMEM((slots, 3) + arrived.shape[1:], jnp.float32),
        pltpu.SMEM((slots, SUBLANES, LANES), jnp.float32),
    ]


def migrate_first(arrived, own, sibling, per_block, samples):
    pieces = math.gcd(own[0].shape[0], 4)
    shape = own[0].shape
    outs = pl.pallas_call(
        functools.partial(first_kernel, arrived.shape[0] // 2, per_block, samples),
        out_shape=[jax.ShapeDtypeStruct((2,) + shape[1:], jnp.float32)]
        + [jax.ShapeDtypeStruct(t.shape, t.dtype) for t in own]
        + [jax.ShapeDtypeStruct((3, 2 * LANES, LANES), jnp.bfloat16)],
        in_specs=[VMEM] + [HBM] * 3 + [VMEM] * 3,
        out_specs=[VMEM] * 5,
        scratch_shapes=migrate_scratch(arrived) + [pltpu.SemaphoreType.DMA((1 + 3 * pieces,))],
        compiler_params=PARAMS,
        cost_estimate=COST,
    )(arrived, *own, *sibling)
    return outs[0], tuple(outs[1:4]), outs[4]


def migrate(arrived, own, sibling, matrix, image, per_block, samples):
    return pl.pallas_call(
        functools.partial(next_kernel, arrived.shape[0] // 2, per_block, samples),
        out_shape=jax.ShapeDtypeStruct(image.shape, jnp.float32),
        in_specs=[VMEM] * 9,
        out_specs=VMEM,
        scratch_shapes=migrate_scratch(arrived) + [pltpu.SemaphoreType.DMA],
        compiler_params=PARAMS,
        cost_estimate=COST,
    )(arrived, *own, *sibling, matrix, image)


def slab_kernel(classes, mine, other, *outs):
    me = lax.axis_index("offs")
    depth = outs[0].shape[0]
    whole = mine[0] + other[...]
    image = outs[-1]
    image[...] = whole
    for k in range(classes):
        outs[k][...] = image[pl.ds((me ^ k) * depth, depth), :]


def slabs(mine, other, classes):
    shape = other.shape
    part = jax.ShapeDtypeStruct((shape[0] // classes, shape[1]), jnp.float32)
    return pl.pallas_call(
        functools.partial(slab_kernel, classes),
        out_shape=[part] * classes,
        in_specs=[VMEM] * 2,
        out_specs=[VMEM] * classes,
        scratch_shapes=[pltpu.VMEM(shape, jnp.float32)],
        compiler_params=PARAMS,
    )(mine, other)


def gather_kernel(classes, *refs):
    out = refs[-1]
    me = lax.axis_index("offs")
    depth = out.shape[1]
    for k in range(classes):
        for d in range(depth):
            out[0, d, pl.ds(me ^ k, 1), :] = refs[k][pl.ds(d, 1), :]


def assemble(parts):
    classes = len(parts)
    depth, cells = parts[0].shape
    return pl.pallas_call(
        functools.partial(gather_kernel, classes),
        out_shape=jax.ShapeDtypeStruct((1, depth, classes, cells), jnp.float32),
        in_specs=[VMEM] * classes,
        out_specs=VMEM,
        compiler_params=PARAMS,
    )(*parts)


def swap(value, axis, k):
    size = lax.axis_size(axis)
    return lax.ppermute(value, axis, [(i, i ^ k) for i in range(size)])


def body(traces, src_node, rec_node, aperture, time_table, amp_table, width_table):
    tiles = lax.axis_size("tile")
    classes = lax.axis_size("offs")
    chips = tiles // 2
    blocks, per_block, samples = traces.shape[1:]
    listed = aperture.shape[2]
    capacity = (3 * blocks * listed + 2 * tiles - 1) // (2 * tiles)
    nodes, _, points = time_table.shape
    own = tuple(t.reshape(nodes, points // LANES, LANES) for t in (time_table, amp_table, width_table))

    packed = pack(src_node, rec_node[0].T, aperture[0].T, traces, chips, capacity)
    arrived = [packed[0]] + [swap(packed[k], "tile", 2 * k) for k in range(1, chips)]
    sibling = tuple(swap(t, "tile", 1) for t in own)
    image, own, matrix = migrate_first(arrived[0], own, sibling, per_block, samples)
    for k in range(1, chips):
        image = migrate(arrived[k], own, sibling, matrix, image, per_block, samples)
    parts = slabs(image, swap(image[1], "tile", 1), classes)
    moved = {0: parts[0]}
    for k in reversed(range(1, classes)):
        moved[k] = swap(parts[k], "offs", k)
    return assemble([moved[k] for k in range(classes)])


def solution(mesh):
    return jax.shard_map(
        body,
        mesh=mesh,
        in_specs=(
            P("offs", "tile", None, None),
            P("offs", "tile"),
            P("offs", "tile", None),
            P("offs", "tile", None),
            P(None, "tile", None),
            P(None, "tile", None),
            P(None, "tile", None),
        ),
        out_specs=P("tile", "offs", None, None),
        check_vma=False,
    )
```

time: 31.5 us -> 31.1 us (0.987)
  Pallas kernels: 12 us -> 11.6 us
    pallas_call x4, Pallas kernels: 10.6 us -> 10.1 us  [the longest x3 7.35 us: migrate(): pl.pallas_call(functools.partial(next_kernel, arrived.shape[0] // 2, per_...]
    unnamed x20 -> x14, local copies, waits for them, and re-layouts: 4.45 us -> 4.44 us
where the time goes in v2:
time: 31.1 us; the launch traced here: 31.3 us
  Pallas kernels  11.6 us (37%)
  starting transfers between devices  9.75 us (31%)
  waiting for transfers between devices  5.4 us (17%)
  local copies, waits for them, and re-layouts  4.45 us (14%)
    ppermute x10, starting transfers between devices, swap(): return lax.ppermute(value, axis, [(i, i ^ k) for i in range(size)])  9.75 us
    pallas_call x3, Pallas kernels, migrate(): pl.pallas_call(functools.partial(next_kernel, arrived.shape[0] // 2, per_...  7.35 us
    ppermute x10, waiting for transfers between devices, swap(): return lax.ppermute(value, axis, [(i, i ^ k) for i in range(size)])  5.4 us
    unnamed x14, local copies, waits for them, and re-layouts  4.44 us
    pallas_call x1, Pallas kernels, migrate_first(): pl.pallas_call(functools.partial(first_kernel, arrived.shape[0] // 2, per...  2.76 us
    pallas_call x1, Pallas kernels, pack(): pl.pallas_call(functools.partial(pack_kernel, chips, capacity), out_shape...  0.84 us
  transfers between devices with their start and end apart: 10, of which 4 were waited for; matrix products, arithmetic and copies ran while one was open for 0% of the time, Pallas kernels for 27%

profile of v2, /device:TPU:0, one launch (start us, length us, event | category | flops | bytes accessed | tf_op | source)
XLA Modules:
  0.0 31.3 jit_solution(17281568520237606693)
XLA Ops:
  0.0 0.5 %collective-permute-start.1 = (s32[32,16,128]{2,1,0:T(8,128)}, s32[32,16,128]{2,1,0:T(8,128)S(1)}, u32[]{:S(2)}, u32[]{:S(2)}) collective-permute-start(s32[32,16,128]{2,1,0:T(8,128)} %bitcast.11), channel_id=1, source_target_pairs={{0,4},{4,0},{8,12},{12,8},{16,20},{20,16},{24,28},{28,24},{1,5},{5... | collective-permute-start | bytes 786440 | tf_op jit(solution)/shard_map/ppermute | solution.py:285
  0.5 0.1 collective-permute-start.2
  0.5 0.5 %collective-permute-start.3 = (s32[32,16,128]{2,1,0:T(8,128)}, s32[32,16,128]{2,1,0:T(8,128)S(1)}, u32[]{:S(2)}, u32[]{:S(2)}) collective-permute-start(s32[32,16,128]{2,1,0:T(8,128)} %bitcast.15), channel_id=1, source_target_pairs={{0,4},{4,0},{8,12},{12,8},{16,20},{20,16},{24,28},{28,24},{1,5},{5... | collective-permute-start | bytes 786440 | tf_op jit(solution)/shard_map/ppermute | solution.py:285
  1.0 0.7 %copy-done.5 = s32[1,8,2]{1,2,0:T(2,128)S(1)} copy-done((s32[1,8,2]{1,2,0:T(2,128)S(1)}, s32[1,8,2]{1,2,0:T(2,128)}, u32[]{:S(2)}) %copy-start.5) | copy-done | bytes 88
  1.7 0.9 %copy-done.3 = f32[1,8,2,2000]{3,2,1,0:T(2,128)S(1)} copy-done((f32[1,8,2,2000]{3,2,1,0:T(2,128)S(1)}, f32[1,8,2,2000]{3,2,1,0:T(2,128)}, u32[]{:S(2)}) %copy-start.3) | copy-done | bytes 128024
  2.6 0.8 %shard_map.73 = (f32[6,32,128]{2,1,0:T(8,128)S(1)}, f32[6,32,128]{2,1,0:T(8,128)S(1)}, f32[6,32,128]{2,1,0:T(8,128)S(1)}, f32[6,32,128]{2,1,0:T(8,128)S(1)}) custom-call(s32[1,8]{1,0:T(1,128)S(1)} %copy-done.6, s32[2,8]{1,0:T(2,128)S(1)} %bitcast.17, s32[2,8]{1,0:T(2,128)S(1)} %bitcast.18, f32[1,8,2,2000]{3,2,1,0:T(2,128)S(1)} %copy-done.3), custom_call_target="tpu_custom_call" | custom-call | tf_op jit(solution)/shard_map/pallas_call | solution.py:71
  3.4 2.6 %collective-permute-start.5 = (f32[6,32,128]{2,1,0:T(8,128)S(1)}, f32[6,32,128]{2,1,0:T(8,128)S(1)}, u32[]{:S(2)}, u32[]{:S(2)}) collective-permute-start(f32[6,32,128]{2,1,0:T(8,128)S(1)} %get-tuple-element.25), channel_id=1, source_target_pairs={{0,8},{4,12},{8,0},{12,4},{16,24},{20,28},{24,16},{28,20},{1,9},{5... | collective-permute-start | bytes 294920 | tf_op jit(solution)/shard_map/ppermute | solution.py:285
  6.1 2.6 %collective-permute-start.4 = (f32[6,32,128]{2,1,0:T(8,128)S(1)}, f32[6,32,128]{2,1,0:T(8,128)S(1)}, u32[]{:S(2)}, u32[]{:S(2)}) collective-permute-start(f32[6,32,128]{2,1,0:T(8,128)S(1)} %get-tuple-element.24), channel_id=1, source_target_pairs={{0,16},{4,20},{8,24},{12,28},{16,0},{20,4},{24,8},{28,12},{1,17},{... | collective-permute-start | bytes 294920 | tf_op jit(solution)/shard_map/ppermute | solution.py:285
  8.7 0.9 %copy-done = s32[32,1,2048]{2,1,0:T(1,128)S(1)} copy-done((s32[32,1,2048]{2,1,0:T(1,128)S(1)}, s32[32,1,2048]{2,1,0:T(1,128)}, u32[]{:S(2)}) %copy-start) | copy-done | bytes 262168
  9.6 0.9 %copy-done.1 = f32[32,1,2048]{2,1,0:T(1,128)S(1)} copy-done((f32[32,1,2048]{2,1,0:T(1,128)S(1)}, f32[32,1,2048]{2,1,0:T(1,128)}, u32[]{:S(2)}) %copy-start.1) | copy-done | bytes 262168
  10.6 0.9 %copy-done.2 = s32[32,1,2048]{2,1,0:T(1,128)S(1)} copy-done((s32[32,1,2048]{2,1,0:T(1,128)S(1)}, s32[32,1,2048]{2,1,0:T(1,128)}, u32[]{:S(2)}) %copy-start.2) | copy-done | bytes 262168
  11.5 2.8 %shard_map.74 = (f32[2,16,128]{2,1,0:T(8,128)S(1)}, s32[32,16,128]{2,1,0:T(8,128)S(1)}, f32[32,16,128]{2,1,0:T(8,128)S(1)}, s32[32,16,128]{2,1,0:T(8,128)S(1)}, bf16[3,256,128]{2,1,0:T(8,128)(2,1)S(1)}) custom-call(f32[6,32,128]{2,1,0:T(8,128)S(1)} %get-tuple-element.19.arrived, s32[32,16,128]{2,1,0:T(8,128)S(1)} %bitcast.12, f32[32,16,128]{2,1,0:T(8,128)S(1)} %bitcast.14, ...), custom_call_target="tpu_custom_call" | custom-call | flops 20000000 | bytes 2000000 | tf_op jit(solution)/shard_map/pallas_call | solution.py:213
  14.3 2.5 %shard_map.75.image_in = f32[2,16,128]{2,1,0:T(8,128)S(1)} custom-call(f32[6,32,128]{2,1,0:T(8,128)S(1)} %collective-permute-done.5.arrived, s32[32,16,128]{2,1,0:T(8,128)S(1)} %get-tuple-element.20.own0, f32[32,16,128]{2,1,0:T(8,128)S(1)} %get-tuple-element.21.own1, s32[32,16,128]{2,1,0:T(8,128)S(1)} %get-tuple-element.22.own2, ...), custom_call_target="tpu_custom_call" | custom-call | flops 20000000 | bytes 2000000 | tf_op jit(solution)/shard_map/pallas_call | solution.py:228
  16.8 2.4 %shard_map.76.image_in = f32[2,16,128]{2,1,0:T(8,128)S(1)} custom-call(f32[6,32,128]{2,1,0:T(8,128)S(1)} %collective-permute-done.4.arrived, s32[32,16,128]{2,1,0:T(8,128)S(1)} %get-tuple-element.20.own0, f32[32,16,128]{2,1,0:T(8,128)S(1)} %get-tuple-element.21.own1, s32[32,16,128]{2,1,0:T(8,128)S(1)} %get-tuple-element.22.own2, ...), custom_call_target="tpu_custom_call" | custom-call | flops 20000000 | bytes 2000000 | tf_op jit(solution)/shard_map/pallas_call | solution.py:228
  19.3 2.5 %shard_map.77.mine = f32[2,16,128]{2,1,0:T(8,128)S(1)} custom-call(f32[6,32,128]{2,1,0:T(8,128)S(1)} %collective-permute-done.arrived, s32[32,16,128]{2,1,0:T(8,128)S(1)} %get-tuple-element.20.own0, f32[32,16,128]{2,1,0:T(8,128)S(1)} %get-tuple-element.21.own1, s32[32,16,128]{2,1,0:T(8,128)S(1)} %get-tuple-element.22.own2, ...), custom_call_target="tpu_custom_call" | custom-call | flops 20000000 | bytes 2000000 | tf_op jit(solution)/shard_map/pallas_call | solution.py:228
  21.7 0.1 collective-permute-start.6
  21.8 1.2 %collective-permute-done.6.other = f32[16,128]{1,0:T(8,128)S(1)} collective-permute-done((f32[16,128]{1,0:T(8,128)S(1)}, f32[16,128]{1,0:T(8,128)S(1)}, u32[]{:S(2)}, u32[]{:S(2)}) %collective-permute-start.6) | collective-permute-done | bytes 8224 | tf_op jit(solution)/shard_map/ppermute | solution.py:285
  23.0 1.7 %collective-permute-start.7 = (f32[4,128]{1,0:T(4,128)S(1)}, f32[4,128]{1,0:T(4,128)S(1)}, u32[]{:S(2)}, u32[]{:S(2)}) collective-permute-start(f32[4,128]{1,0:T(4,128)S(1)} %get-tuple-element.28), channel_id=1, source_target_pairs={{0,1},{1,0},{2,3},{3,2},{4,5},{5,4},{6,7},{7,6},{8,9},{9,8},{10,11... | collective-permute-start | bytes 6152 | tf_op jit(solution)/shard_map/ppermute | solution.py:285
  24.7 1.5 %collective-permute-start.8 = (f32[4,128]{1,0:T(4,128)S(1)}, f32[4,128]{1,0:T(4,128)S(1)}, u32[]{:S(2)}, u32[]{:S(2)}) collective-permute-start(f32[4,128]{1,0:T(4,128)S(1)} %get-tuple-element.29), channel_id=1, source_target_pairs={{0,2},{1,3},{2,0},{3,1},{4,6},{5,7},{6,4},{7,5},{8,10},{9,11},{10,... | collective-permute-start | bytes 6152 | tf_op jit(solution)/shard_map/ppermute | solution.py:285
  26.2 0.3 collective-permute-start.9
  26.5 0.1 collective-permute-done.7.refs_1_
  26.6 1.7 %collective-permute-done.8.refs_2_ = f32[4,128]{1,0:T(4,128)S(1)} collective-permute-done((f32[4,128]{1,0:T(4,128)S(1)}, f32[4,128]{1,0:T(4,128)S(1)}, u32[]{:S(2)}, u32[]{:S(2)}) %collective-permute-start.8) | collective-permute-done | bytes 2080 | tf_op jit(solution)/shard_map/ppermute | solution.py:285
  28.2 2.4 %collective-permute-done.9.refs_3_ = f32[4,128]{1,0:T(4,128)S(1)} collective-permute-done((f32[4,128]{1,0:T(4,128)S(1)}, f32[4,128]{1,0:T(4,128)S(1)}, u32[]{:S(2)}, u32[]{:S(2)}) %collective-permute-start.9) | collective-permute-done | bytes 2080 | tf_op jit(solution)/shard_map/ppermute | solution.py:285
  30.7 0.6 %shard_map.79 = f32[1,4,4,128]{3,2,1,0:T(4,128)} custom-call(f32[4,128]{1,0:T(4,128)S(1)} %get-tuple-element.27.refs_0_, f32[4,128]{1,0:T(4,128)S(1)} %collective-permute-done.7.refs_1_, f32[4,128]{1,0:T(4,128)S(1)} %collective-permute-done.8.refs_2_, f32[4,128]{1,0:T(4,128)S(1)} %collective-permute-done.9.refs_3_), custom_call_target="tpu_custom_call" | custom-call | tf_op jit(solution)/shard_map/pallas_call | solution.py:274
  (18 shorter events, 0.1 us)
Async XLA Ops:
  0.0 8.6 %collective-permute-start.1 = (s32[32,16,128]{2,1,0:T(8,128)}, s32[32,16,128]{2,1,0:T(8,128)S(1)}, u32[]{:S(2)}, u32[]{:S(2)}) collective-permute-start(s32[32,16,128]{2,1,0:T(8,128)} %bitcast.11), channel_id=1, source_target_pairs={{0,4},{4,0},{8,12},{12,8},{16,20},{20,16},{24,28},{28,24},{1,5},{5... | collective-permute-start | bytes 786440 | tf_op jit(solution)/shard_map/ppermute | solution.py:285
  0.5 8.2 %collective-permute-start.2 = (f32[32,16,128]{2,1,0:T(8,128)}, f32[32,16,128]{2,1,0:T(8,128)S(1)}, u32[]{:S(2)}, u32[]{:S(2)}) collective-permute-start(f32[32,16,128]{2,1,0:T(8,128)} %bitcast.13), channel_id=1, source_target_pairs={{0,4},{4,0},{8,12},{12,8},{16,20},{20,16},{24,28},{28,24},{1,5},{5... | collective-permute-start | bytes 786440 | tf_op jit(solution)/shard_map/ppermute | solution.py:285
  0.5 8.1 %collective-permute-start.3 = (s32[32,16,128]{2,1,0:T(8,128)}, s32[32,16,128]{2,1,0:T(8,128)S(1)}, u32[]{:S(2)}, u32[]{:S(2)}) collective-permute-start(s32[32,16,128]{2,1,0:T(8,128)} %bitcast.15), channel_id=1, source_target_pairs={{0,4},{4,0},{8,12},{12,8},{16,20},{20,16},{24,28},{28,24},{1,5},{5... | collective-permute-start | bytes 786440 | tf_op jit(solution)/shard_map/ppermute | solution.py:285
  1.0 0.7 %copy-start.5 = (s32[1,8,2]{1,2,0:T(2,128)S(1)}, s32[1,8,2]{1,2,0:T(2,128)}, u32[]{:S(2)}) copy-start(s32[1,8,2]{1,2,0:T(2,128)} %param.10) | copy-start | bytes 196
  1.0 0.7 %copy-start.4 = (s32[1,8,2]{1,2,0:T(2,128)S(1)}, s32[1,8,2]{1,2,0:T(2,128)}, u32[]{:S(2)}) copy-start(s32[1,8,2]{1,2,0:T(2,128)} %param.9) | copy-start | bytes 196
  1.0 0.7 %copy-start.6 = (s32[1,8]{1,0:T(1,128)S(1)}, s32[1,8]{1,0:T(1,128)}, u32[]{:S(2)}) copy-start(s32[1,8]{1,0:T(1,128)} %src_in.1) | copy-start | bytes 100
  1.7 0.9 %copy-start.3 = (f32[1,8,2,2000]{3,2,1,0:T(2,128)S(1)}, f32[1,8,2,2000]{3,2,1,0:T(2,128)}, u32[]{:S(2)}) copy-start(f32[1,8,2,2000]{3,2,1,0:T(2,128)} %traces_in.1) | copy-start | bytes 384004
  3.4 10.9 %collective-permute-start.5 = (f32[6,32,128]{2,1,0:T(8,128)S(1)}, f32[6,32,128]{2,1,0:T(8,128)S(1)}, u32[]{:S(2)}, u32[]{:S(2)}) collective-permute-start(f32[6,32,128]{2,1,0:T(8,128)S(1)} %get-tuple-element.25), channel_id=1, source_target_pairs={{0,8},{4,12},{8,0},{12,4},{16,24},{20,28},{24,16},{28,20},{1,9},{5... | collective-permute-start | bytes 294920 | tf_op jit(solution)/shard_map/ppermute | solution.py:285
  6.1 10.7 %collective-permute-start.4 = (f32[6,32,128]{2,1,0:T(8,128)S(1)}, f32[6,32,128]{2,1,0:T(8,128)S(1)}, u32[]{:S(2)}, u32[]{:S(2)}) collective-permute-start(f32[6,32,128]{2,1,0:T(8,128)S(1)} %get-tuple-element.24), channel_id=1, source_target_pairs={{0,16},{4,20},{8,24},{12,28},{16,0},{20,4},{24,8},{28,12},{1,17},{... | collective-permute-start | bytes 294920 | tf_op jit(solution)/shard_map/ppermute | solution.py:285
  8.6 10.6 %collective-permute-start = (f32[6,32,128]{2,1,0:T(8,128)S(1)}, f32[6,32,128]{2,1,0:T(8,128)S(1)}, u32[]{:S(2)}, u32[]{:S(2)}) collective-permute-start(f32[6,32,128]{2,1,0:T(8,128)S(1)} %get-tuple-element.18), channel_id=1, source_target_pairs={{0,24},{4,28},{8,16},{12,20},{16,8},{20,12},{24,0},{28,4},{1,25},{... | collective-permute-start | bytes 294920 | tf_op jit(solution)/shard_map/ppermute | solution.py:285
  8.7 1.0 %copy-start = (s32[32,1,2048]{2,1,0:T(1,128)S(1)}, s32[32,1,2048]{2,1,0:T(1,128)}, u32[]{:S(2)}) copy-start(s32[32,1,2048]{2,1,0:T(1,128)} %param.11) | copy-start | bytes 786436
  9.6 0.9 %copy-start.1 = (f32[32,1,2048]{2,1,0:T(1,128)S(1)}, f32[32,1,2048]{2,1,0:T(1,128)}, u32[]{:S(2)}) copy-start(f32[32,1,2048]{2,1,0:T(1,128)} %param.12) | copy-start | bytes 786436
  10.6 0.9 %copy-start.2 = (s32[32,1,2048]{2,1,0:T(1,128)S(1)}, s32[32,1,2048]{2,1,0:T(1,128)}, u32[]{:S(2)}) copy-start(s32[32,1,2048]{2,1,0:T(1,128)} %param.13) | copy-start | bytes 786436
  21.7 1.2 %collective-permute-start.6 = (f32[16,128]{1,0:T(8,128)S(1)}, f32[16,128]{1,0:T(8,128)S(1)}, u32[]{:S(2)}, u32[]{:S(2)}) collective-permute-start(f32[16,128]{1,0:T(8,128)S(1)} %slice_bitcast_fusion), channel_id=1, source_target_pairs={{0,4},{4,0},{8,12},{12,8},{16,20},{20,16},{24,28},{28,24},{1,5},{5... | collective-permute-start | bytes 24584 | tf_op jit(solution)/shard_map/ppermute | solution.py:285
  23.0 3.6 %collective-permute-start.7 = (f32[4,128]{1,0:T(4,128)S(1)}, f32[4,128]{1,0:T(4,128)S(1)}, u32[]{:S(2)}, u32[]{:S(2)}) collective-permute-start(f32[4,128]{1,0:T(4,128)S(1)} %get-tuple-element.28), channel_id=1, source_target_pairs={{0,1},{1,0},{2,3},{3,2},{4,5},{5,4},{6,7},{7,6},{8,9},{9,8},{10,11... | collective-permute-start | bytes 6152 | tf_op jit(solution)/shard_map/ppermute | solution.py:285
  24.7 3.6 %collective-permute-start.8 = (f32[4,128]{1,0:T(4,128)S(1)}, f32[4,128]{1,0:T(4,128)S(1)}, u32[]{:S(2)}, u32[]{:S(2)}) collective-permute-start(f32[4,128]{1,0:T(4,128)S(1)} %get-tuple-element.29), channel_id=1, source_target_pairs={{0,2},{1,3},{2,0},{3,1},{4,6},{5,7},{6,4},{7,5},{8,10},{9,11},{10,... | collective-permute-start | bytes 6152 | tf_op jit(solution)/shard_map/ppermute | solution.py:285
  26.2 4.5 %collective-permute-start.9 = (f32[4,128]{1,0:T(4,128)S(1)}, f32[4,128]{1,0:T(4,128)S(1)}, u32[]{:S(2)}, u32[]{:S(2)}) collective-permute-start(f32[4,128]{1,0:T(4,128)S(1)} %get-tuple-element.30), channel_id=1, source_target_pairs={{0,3},{1,2},{2,1},{3,0},{4,7},{5,6},{6,5},{7,4},{8,11},{9,10},{10,... | collective-permute-start | bytes 6152 | tf_op jit(solution)/shard_map/ppermute | solution.py:285

commit v3 on v2

v3 whole, which is shorter than its diff:
```python
import functools
import math

import jax
import jax.numpy as jnp
from jax import lax
from jax.experimental import pallas as pl
from jax.experimental.pallas import tpu as pltpu
from jax.sharding import PartitionSpec as P

LANES = 128
SUBLANES = 8
VMEM = pl.BlockSpec(memory_space=pltpu.VMEM)
HBM = pl.BlockSpec(memory_space=pltpu.HBM)
PARAMS = pltpu.CompilerParams(vmem_limit_bytes=24 << 20)


def send_orders(chips):
    far = list(range(2, chips))
    return far[:1] + [1] + far[1:], far[::-1][:1] + [1] + far[::-1][1:]


def swap_chips(value, n, chips):
    orders = send_orders(chips)
    return lax.ppermute(value, "tile", [(i, i ^ (2 * orders[i & 1][n])) for i in range(2 * chips)])


def pack_kernel(chips, capacity, src_in, rec_in, ap_in, traces_in, *rest):
    outs = rest[:chips]
    src, rec, ap, traces, block_of, count, sems = rest[chips:]
    copies = [
        pltpu.make_async_copy(a, b, sems.at[n])
        for n, (a, b) in enumerate(((ap_in, ap), (src_in, src), (rec_in, rec)))
    ]
    blocks, per_block, samples = traces.shape
    pieces = sems.shape[0] - 3
    size = blocks // pieces
    for n in range(pieces):
        part = pl.ds(n * size, size)
        copies.append(pltpu.make_async_copy(traces_in.at[0, part], traces.at[part], sems.at[3 + n]))
    for copy in copies:
        copy.start()
    listed = ap.shape[0]
    me = lax.axis_index("tile")
    z, core = me >> 1, me & 1
    for n in range(2 * chips):
        count[n] = 0
    for n in range(2 * chips * capacity):
        block_of[n] = -1
    copies[0].wait()
    for b in range(blocks):
        for e in range(listed):
            tile = ap[e, b]
            group = ((tile >> 1) ^ z) * 2 + ((tile & 1) ^ core)
            place = count[group]
            count[group] = place + 1
            block_of[group * capacity + place] = b
    for copy in copies[1:]:
        copy.wait()
    full, tail = samples // LANES, samples % LANES
    lane = lax.broadcasted_iota(jnp.int32, (per_block, LANES), 1)
    orders = send_orders(chips)
    for n in range(chips):
        k = 0 if n == 0 else jnp.where(core == 0, orders[0][n - 1], orders[1][n - 1])
        for slot in range(2 * capacity):
            b = block_of[k * 2 * capacity + slot]
            live = b >= 0
            b = jnp.maximum(b, 0)
            for h in range(full):
                outs[n][slot, per_block * h:per_block * (h + 1), :] = traces[b, :, h * LANES:(h + 1) * LANES]
            notes = jnp.where(lane == tail, jnp.where(live, src[0, b] + 1, 0), 0)
            for i in range(per_block):
                notes = jnp.where(lane == tail + 1 + i, rec[i, b], notes)
            outs[n][slot, per_block * full:per_block * (full + 1), :] = notes.astype(jnp.float32)
            outs[n][slot, per_block * full:per_block * (full + 1), 0:tail] = traces[b, :, full * LANES:]


def pack(src, rec, ap, traces, chips, capacity):
    blocks, per_block, samples = traces.shape[1:]
    rows = per_block * -(-samples // LANES)
    pieces = math.gcd(blocks, 4)
    return pl.pallas_call(
        functools.partial(pack_kernel, chips, capacity),
        out_shape=[jax.ShapeDtypeStruct((2 * capacity, rows, LANES), jnp.float32)] * chips,
        in_specs=[HBM] * 4,
        out_specs=[VMEM] * chips,
        scratch_shapes=[
            pltpu.SMEM(src.shape, jnp.int32),
            pltpu.SMEM(rec.shape, jnp.int32),
            pltpu.SMEM(ap.shape, jnp.int32),
            pltpu.VMEM(traces.shape[1:], jnp.float32),
            pltpu.SMEM((2 * chips * capacity,), jnp.int32),
            pltpu.SMEM((2 * chips,), jnp.int32),
            pltpu.SemaphoreType.DMA((3 + pieces,)),
        ],
        compiler_params=PARAMS,
    )(*in_hbm(src, rec, ap, traces))


def slots_of(qs, slots):
    return [q * (slots // 2) + j for q in qs for j in range(slots // 2)]


def triangles(x, lane, per_block):
    zero = jnp.zeros((per_block, LANES), jnp.float32)
    after = jnp.concatenate([x[per_block:], zero], 0)
    before = jnp.concatenate([zero, x[:-per_block]], 0)
    pairs = []
    for k in (1, 2, 3, 4):
        ahead = pltpu.roll(jnp.where(lane < k, after, x), LANES - k, 1)
        behind = pltpu.roll(jnp.where(lane >= LANES - k, before, x), k, 1)
        pairs.append(ahead + behind)
    a, b, c, d = pairs
    return (
        0.5 * x + 0.25 * a,
        (3.0 * x + 2.0 * a + b) * (1.0 / 9.0),
        (5.0 * x + 4.0 * a + 3.0 * b + 2.0 * c + d) * (1.0 / 25.0),
    )


def filter_slots(arrived, filtered, per_block, samples, qs):
    slots, rows, _ = arrived.shape
    lane = lax.broadcasted_iota(jnp.int32, (rows, LANES), 1)
    row = lax.broadcasted_iota(jnp.int32, (rows, LANES), 0)
    inside = (row < per_block * (samples // LANES)) | (lane < samples % LANES)
    for slot in slots_of(qs, slots):
        layers = triangles(jnp.where(inside, arrived[slot], 0.0), lane, per_block)
        for c in range(3):
            filtered[slot, c] = layers[c]


def add_slots(q, notes, filtered, tables, image, per_block, samples):
    times, amps, widths = tables
    steps = filtered.shape[2] // per_block
    each = per_block + 1
    capacity = filtered.shape[0] // 2
    live = jnp.int32(0)
    for j in range(capacity):
        live = live + (notes[(q * capacity + j) * each] > 0).astype(jnp.int32)

    def add_slot(j, _):
        slot = q * capacity + j
        s = notes[slot * each] - 1
        for i in range(per_block):
            r = notes[slot * each + 1 + i]
            for half in range(times.shape[1] // SUBLANES):
                part = pl.ds(SUBLANES * half, SUBLANES)
                t = times[s, part] + times[r, part]
                c = jnp.maximum(widths[s, part], widths[r, part])
                weight = amps[s, part] * amps[r, part]
                within = t & (LANES - 1)
                wanted = c * steps + (t >> 7)
                total = None
                for c in range(3):
                    for h in range(steps):
                        line = filtered[slot, c, pl.ds(per_block * h + i, 1), :]
                        got = jnp.take_along_axis(jnp.broadcast_to(line, (SUBLANES, LANES)), within, axis=1)
                        total = got if total is None else jnp.where(wanted == c * steps + h, got, total)
                image[q, part] += weight * total
        return 0

    lax.fori_loop(0, live, add_slot, 0)


def read_notes(arrived, notes, per_block, samples, qs):
    slots, rows, _ = arrived.shape
    tail = samples % LANES
    for slot in slots_of(qs, slots):
        line = arrived[slot, rows - per_block:rows - per_block + 1, :].astype(jnp.int32)
        for i in range(per_block + 1):
            notes[slot * (per_block + 1) + i] = line[0, tail + i]


def first_kernel(
    qs, per_block, samples, arrived, own0, own1, own2, image, times, amps, widths, filtered, notes, sems,
):
    pairs = ((own0, times), (own1, amps), (own2, widths))
    loads = []
    pieces = sems.shape[0] // 3
    size = times.shape[0] // pieces
    for n, (a, b) in enumerate(pairs):
        for m in range(pieces):
            part = pl.ds(m * size, size)
            loads.append(pltpu.make_async_copy(a.at[part], b.at[part], sems.at[n * pieces + m]))
    for load in loads:
        load.start()
    image[...] = jnp.zeros(image.shape, jnp.float32)
    read_notes(arrived, notes, per_block, samples, qs)
    filter_slots(arrived, filtered, per_block, samples, qs)
    for load in loads:
        load.wait()
    for q in qs:
        add_slots(q, notes, filtered, (times, amps, widths), image, per_block, samples)


def next_kernel(
    qs, per_block, samples, arrived, own0, own1, own2, sib0, sib1, sib2, image_in, image, filtered, notes,
):
    read_notes(arrived, notes, per_block, samples, qs)
    filter_slots(arrived, filtered, per_block, samples, qs)
    image[...] = image_in[...]
    for q in qs:
        add_slots(q, notes, filtered, ((own0, own1, own2), (sib0, sib1, sib2))[q], image, per_block, samples)


COST = pl.CostEstimate(flops=20_000_000, bytes_accessed=2_000_000, transcendentals=0)


def migrate_scratch(arrived, per_block):
    slots = arrived.shape[0]
    return [
        pltpu.VMEM((slots, 3) + arrived.shape[1:], jnp.float32),
        pltpu.SMEM((slots * (per_block + 1),), jnp.int32),
    ]


def in_hbm(*arrays):
    return [pltpu.with_memory_space_constraint(a, pltpu.HBM) for a in arrays]


def migrate_first(arrived, own, qs, per_block, samples):
    pieces = math.gcd(own[0].shape[0], 4)
    shape = own[0].shape
    outs = pl.pallas_call(
        functools.partial(first_kernel, qs, per_block, samples),
        out_shape=[jax.ShapeDtypeStruct((2,) + shape[1:], jnp.float32)]
        + [jax.ShapeDtypeStruct(t.shape, t.dtype) for t in own],
        in_specs=[VMEM] + [HBM] * 3,
        out_specs=[VMEM] * 4,
        scratch_shapes=migrate_scratch(arrived, per_block) + [pltpu.SemaphoreType.DMA((3 * pieces,))],
        compiler_params=PARAMS,
        cost_estimate=COST,
    )(arrived, *in_hbm(*own))
    return outs[0], tuple(outs[1:4])


def migrate(arrived, own, sibling, image, qs, per_block, samples):
    return pl.pallas_call(
        functools.partial(next_kernel, qs, per_block, samples),
        out_shape=jax.ShapeDtypeStruct(image.shape, jnp.float32),
        in_specs=[VMEM] * 8,
        out_specs=VMEM,
        scratch_shapes=migrate_scratch(arrived, per_block),
        compiler_params=PARAMS,
        cost_estimate=COST,
    )(arrived, *own, *sibling, image)


def slab_kernel(classes, mine, other, *outs):
    me = lax.axis_index("offs")
    depth = outs[0].shape[0]
    whole = mine[0] + other[...]
    image = outs[-1]
    image[...] = whole
    for k in range(classes):
        outs[k][...] = image[pl.ds((me ^ k) * depth, depth), :]


def slabs(mine, other, classes):
    shape = other.shape
    part = jax.ShapeDtypeStruct((shape[0] // classes, shape[1]), jnp.float32)
    return pl.pallas_call(
        functools.partial(slab_kernel, classes),
        out_shape=[part] * classes,
        in_specs=[VMEM] * 2,
        out_specs=[VMEM] * classes,
        scratch_shapes=[pltpu.VMEM(shape, jnp.float32)],
        compiler_params=PARAMS,
    )(mine, other)


def gather_kernel(classes, *refs):
    out = refs[-1]
    me = lax.axis_index("offs")
    depth = out.shape[1]
    for k in range(classes):
        for d in range(depth):
            out[0, d, pl.ds(me ^ k, 1), :] = refs[k][pl.ds(d, 1), :]


def assemble(parts):
    classes = len(parts)
    depth, cells = parts[0].shape
    return pl.pallas_call(
        functools.partial(gather_kernel, classes),
        out_shape=jax.ShapeDtypeStruct((1, depth, classes, cells), jnp.float32),
        in_specs=[VMEM] * classes,
        out_specs=VMEM,
        compiler_params=PARAMS,
    )(*parts)


def swap(value, axis, k):
    size = lax.axis_size(axis)
    return lax.ppermute(value, axis, [(i, i ^ k) for i in range(size)])


def body(traces, src_node, rec_node, aperture, time_table, amp_table, width_table):
    tiles = lax.axis_size("tile")
    classes = lax.axis_size("offs")
    chips = tiles // 2
    blocks, per_block, samples = traces.shape[1:]
    listed = aperture.shape[2]
    capacity = (3 * blocks * listed + 2 * tiles - 1) // (2 * tiles)
    nodes, _, points = time_table.shape
    own = tuple(t.reshape(nodes, points // LANES, LANES) for t in (time_table, amp_table, width_table))

    packed = pack(src_node, rec_node[0].T, aperture[0].T, traces, chips, capacity)
    arrived = [packed[0]] + [swap_chips(packed[1 + n], n, chips) for n in range(chips - 1)]
    sibling = tuple(swap(t, "tile", 1) for t in lax.optimization_barrier((own, packed[-1]))[0])
    image, own = migrate_first(arrived[0], own, (0,), per_block, samples)
    image = migrate(arrived[0], own, sibling, image, (1,), per_block, samples)
    image = migrate(arrived[1], own, sibling, image, (1, 0), per_block, samples)
    for k in range(2, chips - 1):
        image = migrate(arrived[k], own, sibling, image, (1, 0), per_block, samples)
    image = migrate(arrived[-1], own, sibling, image, (1,), per_block, samples)
    other = swap(image[1], "tile", 1)
    image = migrate(arrived[-1], own, sibling, image, (0,), per_block, samples)
    parts = slabs(image, other, classes)
    return assemble([parts[0]] + [swap(parts[k], "offs", k) for k in range(1, classes)])


def solution(mesh):
    return jax.shard_map(
        body,
        mesh=mesh,
        in_specs=(
            P("offs", "tile", None, None),
            P("offs", "tile"),
            P("offs", "tile", None),
            P("offs", "tile", None),
            P(None, "tile", None),
            P(None, "tile", None),
            P(None, "tile", None),
        ),
        out_specs=P("tile", "offs", None, None),
        check_vma=False,
    )
```

time: 31.1 us -> 25 us (0.80); the launches traced: 31.3 us -> 24.6 us
  local copies, waits for them, and re-layouts: 4.45 us -> 0.01 us
  Pallas kernels: 11.6 us -> 7.59 us
  starting transfers between devices: 9.75 us -> 11 us
  waiting for transfers between devices: 5.4 us -> 5.94 us
    ppermute x0 -> x3, starting transfers between devices: none -> 5.83 us  [swap_chips(): lax.ppermute(value, 'tile', [(i, i ^ 2 * orders[i & 1][n]) for i in range...]
    ppermute x10 -> x7, starting transfers between devices: 9.75 us -> 5.13 us  [swap(): return lax.ppermute(value, axis, [(i, i ^ k) for i in range(size)])]
    unnamed x14 -> x0, local copies, waits for them, and re-layouts: 4.44 us -> none
    pallas_call x4 -> x6, Pallas kernels: 10.1 us -> 5.98 us  [the longest x5 4.35 us: migrate(): pl.pallas_call(functools.partial(next_kernel, qs, per_block, samples), ou...]
    ppermute x0 -> x3, waiting for transfers between devices: none -> 1.78 us  [swap_chips(): lax.ppermute(value, 'tile', [(i, i ^ 2 * orders[i & 1][n]) for i in range...]
    ppermute x10 -> x7, waiting for transfers between devices: 5.4 us -> 4.16 us  [swap(): return lax.ppermute(value, axis, [(i, i ^ k) for i in range(size)])]
  transfers between devices with their start and end apart: 10 -> 10, of which waited for: 4 -> 6; matrix products, arithmetic and copies ran while one was open for 0% -> 0% of each run, Pallas kernels for 27% -> 21%
where the time goes in v3:
time: 25 us; the launch traced here: 24.6 us
  starting transfers between devices  11 us (44%)
  Pallas kernels  7.59 us (30%)
  waiting for transfers between devices  5.94 us (24%)
    ppermute x3, starting transfers between devices, swap_chips(): lax.ppermute(value, 'tile', [(i, i ^ 2 * orders[i & 1][n]) for i in range...  5.83 us
    ppermute x7, starting transfers between devices, swap(): return lax.ppermute(value, axis, [(i, i ^ k) for i in range(size)])  5.13 us
    pallas_call x5, Pallas kernels, migrate(): pl.pallas_call(functools.partial(next_kernel, qs, per_block, samples), ou...  4.35 us
    ppermute x7, waiting for transfers between devices, swap(): return lax.ppermute(value, axis, [(i, i ^ k) for i in range(size)])  4.16 us
    ppermute x3, waiting for transfers between devices, swap_chips(): lax.ppermute(value, 'tile', [(i, i ^ 2 * orders[i & 1][n]) for i in range...  1.78 us
    pallas_call x1, Pallas kernels, migrate_first(): pl.pallas_call(functools.partial(first_kernel, qs, per_block, samples), o...  1.63 us
    pallas_call x1, Pallas kernels, pack(): pl.pallas_call(functools.partial(pack_kernel, chips, capacity), out_shape...  0.99 us
    pallas_call x1, Pallas kernels, assemble(): pl.pallas_call(functools.partial(gather_kernel, classes), out_shape=jax.S...  0.61 us
  transfers between devices with their start and end apart: 10, of which 6 were waited for; matrix products, arithmetic and copies ran while one was open for 0% of the time, Pallas kernels for 21%

profile of v3, /device:TPU:0, one launch (start us, length us, event | category | flops | bytes accessed | tf_op | source)
XLA Modules:
  0.0 24.6 jit_solution(1160430455065569919)
XLA Ops:
  0.0 1.0 %shard_map.73 = (f32[6,32,128]{2,1,0:T(8,128)S(1)}, f32[6,32,128]{2,1,0:T(8,128)S(1)}, f32[6,32,128]{2,1,0:T(8,128)S(1)}, f32[6,32,128]{2,1,0:T(8,128)S(1)}) custom-call(s32[1,8]{1,0:T(1,128)} %src_in.1, s32[2,8]{1,0:T(2,128)} %bitcast.17, s32[2,8]{1,0:T(2,128)} %bitcast.18, f32[1,8,2,2000]{3,2,1,0:T(2,128)} %traces_in.1), custom_call_target="tpu_custom_call" | custom-call | tf_op jit(solution)/shard_map/pallas_call | solution.py:82
  1.0 0.5 %collective-permute-start.1 = (s32[32,16,128]{2,1,0:T(8,128)}, s32[32,16,128]{2,1,0:T(8,128)S(1)}, u32[]{:S(2)}, u32[]{:S(2)}) collective-permute-start(s32[32,16,128]{2,1,0:T(8,128)} %bitcast.11), channel_id=1, source_target_pairs={{0,4},{4,0},{8,12},{12,8},{16,20},{20,16},{24,28},{28,24},{1,5},{5... | collective-permute-start | bytes 786440 | tf_op jit(solution)/shard_map/ppermute | solution.py:295
  1.5 0.1 collective-permute-start.2
  1.6 0.4 %collective-permute-start.3 = (s32[32,16,128]{2,1,0:T(8,128)}, s32[32,16,128]{2,1,0:T(8,128)S(1)}, u32[]{:S(2)}, u32[]{:S(2)}) collective-permute-start(s32[32,16,128]{2,1,0:T(8,128)} %bitcast.15), channel_id=1, source_target_pairs={{0,4},{4,0},{8,12},{12,8},{16,20},{20,16},{24,28},{28,24},{1,5},{5... | collective-permute-start | bytes 786440 | tf_op jit(solution)/shard_map/ppermute | solution.py:295
  2.0 3.7 %collective-permute-start.5 = (f32[6,32,128]{2,1,0:T(8,128)S(1)}, f32[6,32,128]{2,1,0:T(8,128)S(1)}, u32[]{:S(2)}, u32[]{:S(2)}) collective-permute-start(f32[6,32,128]{2,1,0:T(8,128)S(1)} %get-tuple-element.29), channel_id=1, source_target_pairs={{0,16},{4,28},{8,24},{12,20},{16,0},{20,12},{24,8},{28,4},{1,17},{... | collective-permute-start | bytes 294920 | tf_op jit(solution)/shard_map/ppermute | solution.py:25
  5.7 1.6 %collective-permute-start.4 = (f32[6,32,128]{2,1,0:T(8,128)S(1)}, f32[6,32,128]{2,1,0:T(8,128)S(1)}, u32[]{:S(2)}, u32[]{:S(2)}) collective-permute-start(f32[6,32,128]{2,1,0:T(8,128)S(1)} %get-tuple-element.28), channel_id=1, source_target_pairs={{0,8},{4,12},{8,0},{12,4},{16,24},{20,28},{24,16},{28,20},{1,9},{5... | collective-permute-start | bytes 294920 | tf_op jit(solution)/shard_map/ppermute | solution.py:25
  7.3 0.6 %collective-permute-start = (f32[6,32,128]{2,1,0:T(8,128)S(1)}, f32[6,32,128]{2,1,0:T(8,128)S(1)}, u32[]{:S(2)}, u32[]{:S(2)}) collective-permute-start(f32[6,32,128]{2,1,0:T(8,128)S(1)} %get-tuple-element.20), channel_id=1, source_target_pairs={{0,24},{4,20},{8,16},{12,28},{16,8},{20,4},{24,0},{28,12},{1,25},{... | collective-permute-start | bytes 294920 | tf_op jit(solution)/shard_map/ppermute | solution.py:25
  7.9 1.6 %shard_map.74 = (f32[2,16,128]{2,1,0:T(8,128)S(1)}, s32[32,16,128]{2,1,0:T(8,128)S(1)}, f32[32,16,128]{2,1,0:T(8,128)S(1)}, s32[32,16,128]{2,1,0:T(8,128)S(1)}) custom-call(f32[6,32,128]{2,1,0:T(8,128)S(1)} %get-tuple-element.21.arrived, s32[32,16,128]{2,1,0:T(8,128)} %bitcast.12, f32[32,16,128]{2,1,0:T(8,128)} %bitcast.14, s32[32,16,128]{2,1,0:T(8,128)} %bitcast.16), custom_call_target="tpu_custom_call" | custom-call | flops 20000000 | bytes 2000000 | tf_op jit(solution)/shard_map/pallas_call | solution.py:224
  9.5 0.8 %shard_map.75.image_in = f32[2,16,128]{2,1,0:T(8,128)S(1)} custom-call(f32[6,32,128]{2,1,0:T(8,128)S(1)} %get-tuple-element.21.arrived, s32[32,16,128]{2,1,0:T(8,128)S(1)} %get-tuple-element.22.own0, f32[32,16,128]{2,1,0:T(8,128)S(1)} %get-tuple-element.23.own1, s32[32,16,128]{2,1,0:T(8,128)S(1)} %get-tuple-element.24.own2, ...), custom_call_target="tpu_custom_call" | custom-call | flops 20000000 | bytes 2000000 | tf_op jit(solution)/shard_map/pallas_call | solution.py:238
  10.3 1.3 %collective-permute-done.5.arrived = f32[6,32,128]{2,1,0:T(8,128)S(1)} collective-permute-done((f32[6,32,128]{2,1,0:T(8,128)S(1)}, f32[6,32,128]{2,1,0:T(8,128)S(1)}, u32[]{:S(2)}, u32[]{:S(2)}) %collective-permute-start.5) | collective-permute-done | bytes 98336 | tf_op jit(solution)/shard_map/ppermute | solution.py:25
  11.6 1.2 %shard_map.76.image_in = f32[2,16,128]{2,1,0:T(8,128)S(1)} custom-call(f32[6,32,128]{2,1,0:T(8,128)S(1)} %collective-permute-done.5.arrived, s32[32,16,128]{2,1,0:T(8,128)S(1)} %get-tuple-element.22.own0, f32[32,16,128]{2,1,0:T(8,128)S(1)} %get-tuple-element.23.own1, s32[32,16,128]{2,1,0:T(8,128)S(1)} %get-tuple-element.24.own2, ...), custom_call_target="tpu_custom_call" | custom-call | flops 20000000 | bytes 2000000 | tf_op jit(solution)/shard_map/pallas_call | solution.py:238
  12.7 1.2 %shard_map.77.image_in = f32[2,16,128]{2,1,0:T(8,128)S(1)} custom-call(f32[6,32,128]{2,1,0:T(8,128)S(1)} %collective-permute-done.4.arrived, s32[32,16,128]{2,1,0:T(8,128)S(1)} %get-tuple-element.22.own0, f32[32,16,128]{2,1,0:T(8,128)S(1)} %get-tuple-element.23.own1, s32[32,16,128]{2,1,0:T(8,128)S(1)} %get-tuple-element.24.own2, ...), custom_call_target="tpu_custom_call" | custom-call | flops 20000000 | bytes 2000000 | tf_op jit(solution)/shard_map/pallas_call | solution.py:238
  13.9 0.5 %collective-permute-done.arrived = f32[6,32,128]{2,1,0:T(8,128)S(1)} collective-permute-done((f32[6,32,128]{2,1,0:T(8,128)S(1)}, f32[6,32,128]{2,1,0:T(8,128)S(1)}, u32[]{:S(2)}, u32[]{:S(2)}) %collective-permute-start) | collective-permute-done | bytes 98336 | tf_op jit(solution)/shard_map/ppermute | solution.py:25
  14.5 0.8 %shard_map.78.image_in = f32[2,16,128]{2,1,0:T(8,128)S(1)} custom-call(f32[6,32,128]{2,1,0:T(8,128)S(1)} %collective-permute-done.arrived, s32[32,16,128]{2,1,0:T(8,128)S(1)} %get-tuple-element.22.own0, f32[32,16,128]{2,1,0:T(8,128)S(1)} %get-tuple-element.23.own1, s32[32,16,128]{2,1,0:T(8,128)S(1)} %get-tuple-element.24.own2, ...), custom_call_target="tpu_custom_call" | custom-call | flops 20000000 | bytes 2000000 | tf_op jit(solution)/shard_map/pallas_call | solution.py:238
  15.2 0.6 %collective-permute-start.6 = (f32[16,128]{1,0:T(8,128)S(1)}, f32[16,128]{1,0:T(8,128)S(1)}, u32[]{:S(2)}, u32[]{:S(2)}) collective-permute-start(f32[16,128]{1,0:T(8,128)S(1)} %slice_bitcast_fusion), channel_id=1, source_target_pairs={{0,4},{4,0},{8,12},{12,8},{16,20},{20,16},{24,28},{28,24},{1,5},{5... | collective-permute-start | bytes 24584 | tf_op jit(solution)/shard_map/ppermute | solution.py:295
  15.8 0.5 %shard_map.79.mine = f32[2,16,128]{2,1,0:T(8,128)S(1)} custom-call(f32[6,32,128]{2,1,0:T(8,128)S(1)} %collective-permute-done.arrived, s32[32,16,128]{2,1,0:T(8,128)S(1)} %get-tuple-element.22.own0, f32[32,16,128]{2,1,0:T(8,128)S(1)} %get-tuple-element.23.own1, s32[32,16,128]{2,1,0:T(8,128)S(1)} %get-tuple-element.24.own2, ...), custom_call_target="tpu_custom_call" | custom-call | flops 20000000 | bytes 2000000 | tf_op jit(solution)/shard_map/pallas_call | solution.py:238
  16.3 0.3 %collective-permute-done.6.other = f32[16,128]{1,0:T(8,128)S(1)} collective-permute-done((f32[16,128]{1,0:T(8,128)S(1)}, f32[16,128]{1,0:T(8,128)S(1)}, u32[]{:S(2)}, u32[]{:S(2)}) %collective-permute-start.6) | collective-permute-done | bytes 8224 | tf_op jit(solution)/shard_map/ppermute | solution.py:295
  16.7 1.3 %collective-permute-start.7 = (f32[4,128]{1,0:T(4,128)S(1)}, f32[4,128]{1,0:T(4,128)S(1)}, u32[]{:S(2)}, u32[]{:S(2)}) collective-permute-start(f32[4,128]{1,0:T(4,128)S(1)} %get-tuple-element.32), channel_id=1, source_target_pairs={{0,1},{1,0},{2,3},{3,2},{4,5},{5,4},{6,7},{7,6},{8,9},{9,8},{10,11... | collective-permute-start | bytes 6152 | tf_op jit(solution)/shard_map/ppermute | solution.py:295
  18.0 1.5 %collective-permute-start.8 = (f32[4,128]{1,0:T(4,128)S(1)}, f32[4,128]{1,0:T(4,128)S(1)}, u32[]{:S(2)}, u32[]{:S(2)}) collective-permute-start(f32[4,128]{1,0:T(4,128)S(1)} %get-tuple-element.33), channel_id=1, source_target_pairs={{0,2},{1,3},{2,0},{3,1},{4,6},{5,7},{6,4},{7,5},{8,10},{9,11},{10,... | collective-permute-start | bytes 6152 | tf_op jit(solution)/shard_map/ppermute | solution.py:295
  19.5 0.7 %collective-permute-start.9 = (f32[4,128]{1,0:T(4,128)S(1)}, f32[4,128]{1,0:T(4,128)S(1)}, u32[]{:S(2)}, u32[]{:S(2)}) collective-permute-start(f32[4,128]{1,0:T(4,128)S(1)} %get-tuple-element.34), channel_id=1, source_target_pairs={{0,3},{1,2},{2,1},{3,0},{4,7},{5,6},{6,5},{7,4},{8,11},{9,10},{10,... | collective-permute-start | bytes 6152 | tf_op jit(solution)/shard_map/ppermute | solution.py:295
  20.2 0.1 collective-permute-done.7.refs_1_
  20.3 1.3 %collective-permute-done.8.refs_2_ = f32[4,128]{1,0:T(4,128)S(1)} collective-permute-done((f32[4,128]{1,0:T(4,128)S(1)}, f32[4,128]{1,0:T(4,128)S(1)}, u32[]{:S(2)}, u32[]{:S(2)}) %collective-permute-start.8) | collective-permute-done | bytes 2080 | tf_op jit(solution)/shard_map/ppermute | solution.py:295
  21.6 2.4 %collective-permute-done.9.refs_3_ = f32[4,128]{1,0:T(4,128)S(1)} collective-permute-done((f32[4,128]{1,0:T(4,128)S(1)}, f32[4,128]{1,0:T(4,128)S(1)}, u32[]{:S(2)}, u32[]{:S(2)}) %collective-permute-start.9) | collective-permute-done | bytes 2080 | tf_op jit(solution)/shard_map/ppermute | solution.py:295
  24.0 0.6 %shard_map.81 = f32[1,4,4,128]{3,2,1,0:T(4,128)} custom-call(f32[4,128]{1,0:T(4,128)S(1)} %get-tuple-element.31.refs_0_, f32[4,128]{1,0:T(4,128)S(1)} %collective-permute-done.7.refs_1_, f32[4,128]{1,0:T(4,128)S(1)} %collective-permute-done.8.refs_2_, f32[4,128]{1,0:T(4,128)S(1)} %collective-permute-done.9.refs_3_), custom_call_target="tpu_custom_call" | custom-call | tf_op jit(solution)/shard_map/pallas_call | solution.py:284
  (6 shorter events, 0.0 us)
Async XLA Ops:
  1.0 6.3 %collective-permute-start.1 = (s32[32,16,128]{2,1,0:T(8,128)}, s32[32,16,128]{2,1,0:T(8,128)S(1)}, u32[]{:S(2)}, u32[]{:S(2)}) collective-permute-start(s32[32,16,128]{2,1,0:T(8,128)} %bitcast.11), channel_id=1, source_target_pairs={{0,4},{4,0},{8,12},{12,8},{16,20},{20,16},{24,28},{28,24},{1,5},{5... | collective-permute-start | bytes 786440 | tf_op jit(solution)/shard_map/ppermute | solution.py:295
  1.5 8.0 %collective-permute-start.2 = (f32[32,16,128]{2,1,0:T(8,128)}, f32[32,16,128]{2,1,0:T(8,128)S(1)}, u32[]{:S(2)}, u32[]{:S(2)}) collective-permute-start(f32[32,16,128]{2,1,0:T(8,128)} %bitcast.13), channel_id=1, source_target_pairs={{0,4},{4,0},{8,12},{12,8},{16,20},{20,16},{24,28},{28,24},{1,5},{5... | collective-permute-start | bytes 786440 | tf_op jit(solution)/shard_map/ppermute | solution.py:295
  1.6 7.9 %collective-permute-start.3 = (s32[32,16,128]{2,1,0:T(8,128)}, s32[32,16,128]{2,1,0:T(8,128)S(1)}, u32[]{:S(2)}, u32[]{:S(2)}) collective-permute-start(s32[32,16,128]{2,1,0:T(8,128)} %bitcast.15), channel_id=1, source_target_pairs={{0,4},{4,0},{8,12},{12,8},{16,20},{20,16},{24,28},{28,24},{1,5},{5... | collective-permute-start | bytes 786440 | tf_op jit(solution)/shard_map/ppermute | solution.py:295
  2.0 9.5 %collective-permute-start.5 = (f32[6,32,128]{2,1,0:T(8,128)S(1)}, f32[6,32,128]{2,1,0:T(8,128)S(1)}, u32[]{:S(2)}, u32[]{:S(2)}) collective-permute-start(f32[6,32,128]{2,1,0:T(8,128)S(1)} %get-tuple-element.29), channel_id=1, source_target_pairs={{0,16},{4,28},{8,24},{12,20},{16,0},{20,12},{24,8},{28,4},{1,17},{... | collective-permute-start | bytes 294920 | tf_op jit(solution)/shard_map/ppermute | solution.py:25
  5.7 7.0 %collective-permute-start.4 = (f32[6,32,128]{2,1,0:T(8,128)S(1)}, f32[6,32,128]{2,1,0:T(8,128)S(1)}, u32[]{:S(2)}, u32[]{:S(2)}) collective-permute-start(f32[6,32,128]{2,1,0:T(8,128)S(1)} %get-tuple-element.28), channel_id=1, source_target_pairs={{0,8},{4,12},{8,0},{12,4},{16,24},{20,28},{24,16},{28,20},{1,9},{5... | collective-permute-start | bytes 294920 | tf_op jit(solution)/shard_map/ppermute | solution.py:25
  7.3 7.2 %collective-permute-start = (f32[6,32,128]{2,1,0:T(8,128)S(1)}, f32[6,32,128]{2,1,0:T(8,128)S(1)}, u32[]{:S(2)}, u32[]{:S(2)}) collective-permute-start(f32[6,32,128]{2,1,0:T(8,128)S(1)} %get-tuple-element.20), channel_id=1, source_target_pairs={{0,24},{4,20},{8,16},{12,28},{16,8},{20,4},{24,0},{28,12},{1,25},{... | collective-permute-start | bytes 294920 | tf_op jit(solution)/shard_map/ppermute | solution.py:25
  15.2 1.4 %collective-permute-start.6 = (f32[16,128]{1,0:T(8,128)S(1)}, f32[16,128]{1,0:T(8,128)S(1)}, u32[]{:S(2)}, u32[]{:S(2)}) collective-permute-start(f32[16,128]{1,0:T(8,128)S(1)} %slice_bitcast_fusion), channel_id=1, source_target_pairs={{0,4},{4,0},{8,12},{12,8},{16,20},{20,16},{24,28},{28,24},{1,5},{5... | collective-permute-start | bytes 24584 | tf_op jit(solution)/shard_map/ppermute | solution.py:295
  16.7 3.6 %collective-permute-start.7 = (f32[4,128]{1,0:T(4,128)S(1)}, f32[4,128]{1,0:T(4,128)S(1)}, u32[]{:S(2)}, u32[]{:S(2)}) collective-permute-start(f32[4,128]{1,0:T(4,128)S(1)} %get-tuple-element.32), channel_id=1, source_target_pairs={{0,1},{1,0},{2,3},{3,2},{4,5},{5,4},{6,7},{7,6},{8,9},{9,8},{10,11... | collective-permute-start | bytes 6152 | tf_op jit(solution)/shard_map/ppermute | solution.py:295
  18.0 3.6 %collective-permute-start.8 = (f32[4,128]{1,0:T(4,128)S(1)}, f32[4,128]{1,0:T(4,128)S(1)}, u32[]{:S(2)}, u32[]{:S(2)}) collective-permute-start(f32[4,128]{1,0:T(4,128)S(1)} %get-tuple-element.33), channel_id=1, source_target_pairs={{0,2},{1,3},{2,0},{3,1},{4,6},{5,7},{6,4},{7,5},{8,10},{9,11},{10,... | collective-permute-start | bytes 6152 | tf_op jit(solution)/shard_map/ppermute | solution.py:295
  19.5 4.5 %collective-permute-start.9 = (f32[4,128]{1,0:T(4,128)S(1)}, f32[4,128]{1,0:T(4,128)S(1)}, u32[]{:S(2)}, u32[]{:S(2)}) collective-permute-start(f32[4,128]{1,0:T(4,128)S(1)} %get-tuple-element.34), channel_id=1, source_target_pairs={{0,3},{1,2},{2,1},{3,0},{4,7},{5,6},{6,5},{7,4},{8,11},{9,10},{10,... | collective-permute-start | bytes 6152 | tf_op jit(solution)/shard_map/ppermute | solution.py:295

commit v4 on v3

--- a/solution.py
+++ b/solution.py
@@ -15,14 +15,13 @@
 PARAMS = pltpu.CompilerParams(vmem_limit_bytes=24 << 20)
 
 
-def send_orders(chips):
+def send_order(chips):
     far = list(range(2, chips))
-    return far[:1] + [1] + far[1:], far[::-1][:1] + [1] + far[::-1][1:]
+    return far[:1] + [1] + far[1:]
 
 
 def swap_chips(value, n, chips):
-    orders = send_orders(chips)
-    return lax.ppermute(value, "tile", [(i, i ^ (2 * orders[i & 1][n])) for i in range(2 * chips)])
+    return swap(value, "tile", 2 * send_order(chips)[n])
 
 
 def pack_kernel(chips, capacity, src_in, rec_in, ap_in, traces_in, *rest):
@@ -59,9 +58,9 @@
         copy.wait()
     full, tail = samples // LANES, samples % LANES
     lane = lax.broadcasted_iota(jnp.int32, (per_block, LANES), 1)
-    orders = send_orders(chips)
+    distances = [0] + send_order(chips)
     for n in range(chips):
-        k = 0 if n == 0 else jnp.where(core == 0, orders[0][n - 1], orders[1][n - 1])
+        k = distances[n]
         for slot in range(2 * capacity):
             b = block_of[k * 2 * capacity + slot]
             live = b >= 0
@@ -246,48 +245,69 @@
     )(arrived, *own, *sibling, image)
 
 
-def slab_kernel(classes, mine, other, *outs):
+def halve_kernel(distance, counts, *refs):
+    ins, (keep, send) = refs[:-2], refs[-2:]
+    upper = (lax.axis_index("offs") & distance) != 0
+    rows = keep.shape[1]
+    at = 0
+    for ref, count in zip(ins, counts):
+        for j in range(count):
+            low, high = ref[j, :rows], ref[j, rows:]
+            keep[at] = jnp.where(upper, high, low)
+            send[at] = jnp.where(upper, low, high)
+            at += 1
+
+
+def sum_halve_kernel(distance, image, other, keep, send):
+    upper = (lax.axis_index("offs") & distance) != 0
+    rows = keep.shape[1]
+    whole = image[0] + other[...]
+    low, high = whole[:rows], whole[rows:]
+    keep[0] = jnp.where(upper, high, low)
+    send[0] = jnp.where(upper, low, high)
+
+
+def halve(kernel, arrays, held, rows):
+    part = jax.ShapeDtypeStruct((held, rows // 2, LANES), jnp.float32)
+    return pl.pallas_call(
+        kernel,
+        out_shape=[part, part],
+        in_specs=[VMEM] * len(arrays),
+        out_specs=[VMEM] * 2,
+        compiler_params=PARAMS,
+    )(*arrays)
+
+
+def gather_kernel(order, keep, came, out):
     me = lax.axis_index("offs")
-    depth = outs[0].shape[0]
-    whole = mine[0] + other[...]
-    image = outs[-1]
-    image[...] = whole
-    for k in range(classes):
-        outs[k][...] = image[pl.ds((me ^ k) * depth, depth), :]
-
-
-def slabs(mine, other, classes):
-    shape = other.shape
-    part = jax.ShapeDtypeStruct((shape[0] // classes, shape[1]), jnp.float32)
+    held, depth, _ = keep.shape
+    for j, distance in enumerate(order):
+        ref, at = (keep, j) if j < held else (came, j - held)
+        for d in range(depth):
+            out[0, d, pl.ds(me ^ distance, 1), :] = ref[at, pl.ds(d, 1), :]
+
+
+def exchange_slabs(image, other, classes):
+    rows = other.shape[0]
+    distance = classes // 2
+    keep, send = halve(functools.partial(sum_halve_kernel, distance), (image, other), 1, rows)
+    order = [0]
+    while True:
+        came = swap(send, "offs", distance)
+        order = order + [k ^ distance for k in order]
+        rows //= 2
+        distance //= 2
+        if distance == 0:
+            break
+        counts = (len(order) // 2,) * 2
+        keep, send = halve(functools.partial(halve_kernel, distance, counts), (keep, came), len(order), rows)
     return pl.pallas_call(
-        functools.partial(slab_kernel, classes),
-        out_shape=[part] * classes,
+        functools.partial(gather_kernel, order),
+        out_shape=jax.ShapeDtypeStruct((1, rows, classes, LANES), jnp.float32),
         in_specs=[VMEM] * 2,
-        out_specs=[VMEM] * classes,
-        scratch_shapes=[pltpu.VMEM(shape, jnp.float32)],
-        compiler_params=PARAMS,
-    )(mine, other)
-
-
-def gather_kernel(classes, *refs):
-    out = refs[-1]
-    me = lax.axis_index("offs")
-    depth = out.shape[1]
-    for k in range(classes):
-        for d in range(depth):
-            out[0, d, pl.ds(me ^ k, 1), :] = refs[k][pl.ds(d, 1), :]
-
-
-def assemble(parts):
-    classes = len(parts)
-    depth, cells = parts[0].shape
-    return pl.pallas_call(
-        functools.partial(gather_kernel, classes),
-        out_shape=jax.ShapeDtypeStruct((1, depth, classes, cells), jnp.float32),
-        in_specs=[VMEM] * classes,
         out_specs=VMEM,
         compiler_params=PARAMS,
-    )(*parts)
+    )(keep, came)
 
 
 def swap(value, axis, k):
@@ -307,7 +327,7 @@
 
     packed = pack(src_node, rec_node[0].T, aperture[0].T, traces, chips, capacity)
     arrived = [packed[0]] + [swap_chips(packed[1 + n], n, chips) for n in range(chips - 1)]
-    sibling = tuple(swap(t, "tile", 1) for t in lax.optimization_barrier((own, packed[-1]))[0])
+    sibling = tuple(swap(t, "tile", 1) for t in own)
     image, own = migrate_first(arrived[0], own, (0,), per_block, samples)
     image = migrate(arrived[0], own, sibling, image, (1,), per_block, samples)
     image = migrate(arrived[1], own, sibling, image, (1, 0), per_block, samples)
@@ -316,8 +336,7 @@
     image = migrate(arrived[-1], own, sibling, image, (1,), per_block, samples)
     other = swap(image[1], "tile", 1)
     image = migrate(arrived[-1], own, sibling, image, (0,), per_block, samples)
-    parts = slabs(image, other, classes)
-    return assemble([parts[0]] + [swap(parts[k], "offs", k) for k in range(1, classes)])
+    return exchange_slabs(image, other, classes)
 
 
 def solution(mesh):

time: 25 us -> 24.6 us (0.984)
  starting transfers between devices: 11 us -> 9.44 us
  Pallas kernels: 7.59 us -> 8.76 us
    ppermute x3 -> x0, starting transfers between devices: 5.83 us -> none  [swap_chips(): lax.ppermute(value, 'tile', [(i, i ^ 2 * orders[i & 1][n]) for i in range...]
    ppermute x7 -> x9, starting transfers between devices: 5.13 us -> 9.44 us  [swap(): return lax.ppermute(value, axis, [(i, i ^ k) for i in range(size)])]
    ppermute x7 -> x9, waiting for transfers between devices: 4.16 us -> 6.05 us  [swap(): return lax.ppermute(value, axis, [(i, i ^ k) for i in range(size)])]
    ppermute x3 -> x0, waiting for transfers between devices: 1.78 us -> none  [swap_chips(): lax.ppermute(value, 'tile', [(i, i ^ 2 * orders[i & 1][n]) for i in range...]
    pallas_call x5, Pallas kernels: 4.35 us -> 5.23 us  [migrate(): pl.pallas_call(functools.partial(next_kernel, qs, per_block, samples), ou...]
    pallas_call x1, Pallas kernels: 1.63 us -> 1.92 us  [migrate_first(): pl.pallas_call(functools.partial(first_kernel, qs, per_block, samples), o...]
    pallas_call x2 -> x3, Pallas kernels: 0.62 us -> 0.61 us  [the longest x1 0.61 us: exchange_slabs(): pl.pallas_call(functools.partial(gather_kernel, order), out_shape=jax.Sha...]
  transfers between devices with their start and end apart: 10 -> 9, of which waited for: 6 -> 5; matrix products, arithmetic and copies ran while one was open for 0% -> 0% of each run, Pallas kernels for 21% -> 30%
where the time goes in v4:
time: 24.6 us; the launch traced here: 24.4 us
  starting transfers between devices  9.44 us (38%)
  Pallas kernels  8.76 us (36%)
  waiting for transfers between devices  6.05 us (25%)
    ppermute x9, starting transfers between devices, swap(): return lax.ppermute(value, axis, [(i, i ^ k) for i in range(size)])  9.44 us
    ppermute x9, waiting for transfers between devices, swap(): return lax.ppermute(value, axis, [(i, i ^ k) for i in range(size)])  6.05 us
    pallas_call x5, Pallas kernels, migrate(): pl.pallas_call(functools.partial(next_kernel, qs, per_block, samples), ou...  5.23 us
    pallas_call x1, Pallas kernels, migrate_first(): pl.pallas_call(functools.partial(first_kernel, qs, per_block, samples), o...  1.92 us
    pallas_call x1, Pallas kernels, pack(): pl.pallas_call(functools.partial(pack_kernel, chips, capacity), out_shape...  0.98 us
    pallas_call x1, Pallas kernels, exchange_slabs(): pl.pallas_call(functools.partial(gather_kernel, order), out_shape=jax.Sha...  0.61 us
  transfers between devices with their start and end apart: 9, of which 5 were waited for; matrix products, arithmetic and copies ran while one was open for 0% of the time, Pallas kernels for 30%

profile of v4, /device:TPU:0, one launch (start us, length us, event | category | flops | bytes accessed | tf_op | source)
XLA Modules:
  0.0 24.4 jit_solution(14421077935670255252)
XLA Ops:
  0.0 0.5 %collective-permute-start.1 = (s32[32,16,128]{2,1,0:T(8,128)}, s32[32,16,128]{2,1,0:T(8,128)S(1)}, u32[]{:S(2)}, u32[]{:S(2)}) collective-permute-start(s32[32,16,128]{2,1,0:T(8,128)} %bitcast.11), channel_id=1, source_target_pairs={{0,4},{4,0},{8,12},{12,8},{16,20},{20,16},{24,28},{28,24},{1,5},{5... | collective-permute-start | bytes 786440 | tf_op jit(solution)/shard_map/ppermute | solution.py:315
  0.5 0.1 collective-permute-start.2
  0.5 0.5 %collective-permute-start.3 = (s32[32,16,128]{2,1,0:T(8,128)}, s32[32,16,128]{2,1,0:T(8,128)S(1)}, u32[]{:S(2)}, u32[]{:S(2)}) collective-permute-start(s32[32,16,128]{2,1,0:T(8,128)} %bitcast.15), channel_id=1, source_target_pairs={{0,4},{4,0},{8,12},{12,8},{16,20},{20,16},{24,28},{28,24},{1,5},{5... | collective-permute-start | bytes 786440 | tf_op jit(solution)/shard_map/ppermute | solution.py:315
  1.0 1.0 %shard_map.73 = (f32[6,32,128]{2,1,0:T(8,128)S(1)}, f32[6,32,128]{2,1,0:T(8,128)S(1)}, f32[6,32,128]{2,1,0:T(8,128)S(1)}, f32[6,32,128]{2,1,0:T(8,128)S(1)}) custom-call(s32[1,8]{1,0:T(1,128)} %src_in.1, s32[2,8]{1,0:T(2,128)} %bitcast.17, s32[2,8]{1,0:T(2,128)} %bitcast.18, f32[1,8,2,2000]{3,2,1,0:T(2,128)} %traces_in.1), custom_call_target="tpu_custom_call" | custom-call | tf_op jit(solution)/shard_map/pallas_call | solution.py:81
  2.0 3.7 %collective-permute-start.5 = (f32[6,32,128]{2,1,0:T(8,128)S(1)}, f32[6,32,128]{2,1,0:T(8,128)S(1)}, u32[]{:S(2)}, u32[]{:S(2)}) collective-permute-start(f32[6,32,128]{2,1,0:T(8,128)S(1)} %get-tuple-element.23), channel_id=1, source_target_pairs={{0,16},{4,20},{8,24},{12,28},{16,0},{20,4},{24,8},{28,12},{1,17},{... | collective-permute-start | bytes 294920 | tf_op jit(solution)/shard_map/ppermute | solution.py:315
  5.6 1.6 %collective-permute-start.4 = (f32[6,32,128]{2,1,0:T(8,128)S(1)}, f32[6,32,128]{2,1,0:T(8,128)S(1)}, u32[]{:S(2)}, u32[]{:S(2)}) collective-permute-start(f32[6,32,128]{2,1,0:T(8,128)S(1)} %get-tuple-element.22), channel_id=1, source_target_pairs={{0,8},{4,12},{8,0},{12,4},{16,24},{20,28},{24,16},{28,20},{1,9},{5... | collective-permute-start | bytes 294920 | tf_op jit(solution)/shard_map/ppermute | solution.py:315
  7.2 0.0 collective-permute-done.1.sib0
  7.2 0.0 collective-permute-start
  7.2 1.9 %shard_map.74 = (f32[2,16,128]{2,1,0:T(8,128)S(1)}, s32[32,16,128]{2,1,0:T(8,128)S(1)}, f32[32,16,128]{2,1,0:T(8,128)S(1)}, s32[32,16,128]{2,1,0:T(8,128)S(1)}) custom-call(f32[6,32,128]{2,1,0:T(8,128)S(1)} %get-tuple-element.18.arrived, s32[32,16,128]{2,1,0:T(8,128)} %bitcast.12, f32[32,16,128]{2,1,0:T(8,128)} %bitcast.14, s32[32,16,128]{2,1,0:T(8,128)} %bitcast.16), custom_call_target="tpu_custom_call" | custom-call | flops 20000000 | bytes 2000000 | tf_op jit(solution)/shard_map/pallas_call | solution.py:223
  9.1 0.0 collective-permute-done.2.sib1
  9.1 0.8 %shard_map.75.image_in = f32[2,16,128]{2,1,0:T(8,128)S(1)} custom-call(f32[6,32,128]{2,1,0:T(8,128)S(1)} %get-tuple-element.18.arrived, s32[32,16,128]{2,1,0:T(8,128)S(1)} %get-tuple-element.19.own0, f32[32,16,128]{2,1,0:T(8,128)S(1)} %get-tuple-element.20.own1, s32[32,16,128]{2,1,0:T(8,128)S(1)} %get-tuple-element.21.own2, ...), custom_call_target="tpu_custom_call" | custom-call | flops 20000000 | bytes 2000000 | tf_op jit(solution)/shard_map/pallas_call | solution.py:237
  9.9 1.4 %collective-permute-done.5.arrived = f32[6,32,128]{2,1,0:T(8,128)S(1)} collective-permute-done((f32[6,32,128]{2,1,0:T(8,128)S(1)}, f32[6,32,128]{2,1,0:T(8,128)S(1)}, u32[]{:S(2)}, u32[]{:S(2)}) %collective-permute-start.5) | collective-permute-done | bytes 98336 | tf_op jit(solution)/shard_map/ppermute | solution.py:315
  11.4 1.5 %shard_map.76.image_in = f32[2,16,128]{2,1,0:T(8,128)S(1)} custom-call(f32[6,32,128]{2,1,0:T(8,128)S(1)} %collective-permute-done.5.arrived, s32[32,16,128]{2,1,0:T(8,128)S(1)} %get-tuple-element.19.own0, f32[32,16,128]{2,1,0:T(8,128)S(1)} %get-tuple-element.20.own1, s32[32,16,128]{2,1,0:T(8,128)S(1)} %get-tuple-element.21.own2, ...), custom_call_target="tpu_custom_call" | custom-call | flops 20000000 | bytes 2000000 | tf_op jit(solution)/shard_map/pallas_call | solution.py:237
  12.8 1.5 %shard_map.77.image_in = f32[2,16,128]{2,1,0:T(8,128)S(1)} custom-call(f32[6,32,128]{2,1,0:T(8,128)S(1)} %collective-permute-done.4.arrived, s32[32,16,128]{2,1,0:T(8,128)S(1)} %get-tuple-element.19.own0, f32[32,16,128]{2,1,0:T(8,128)S(1)} %get-tuple-element.20.own1, s32[32,16,128]{2,1,0:T(8,128)S(1)} %get-tuple-element.21.own2, ...), custom_call_target="tpu_custom_call" | custom-call | flops 20000000 | bytes 2000000 | tf_op jit(solution)/shard_map/pallas_call | solution.py:237
  14.3 0.2 collective-permute-done.arrived
  14.5 0.8 %shard_map.78.image_in = f32[2,16,128]{2,1,0:T(8,128)S(1)} custom-call(f32[6,32,128]{2,1,0:T(8,128)S(1)} %collective-permute-done.arrived, s32[32,16,128]{2,1,0:T(8,128)S(1)} %get-tuple-element.19.own0, f32[32,16,128]{2,1,0:T(8,128)S(1)} %get-tuple-element.20.own1, s32[32,16,128]{2,1,0:T(8,128)S(1)} %get-tuple-element.21.own2, ...), custom_call_target="tpu_custom_call" | custom-call | flops 20000000 | bytes 2000000 | tf_op jit(solution)/shard_map/pallas_call | solution.py:237
  15.3 0.1 collective-permute-start.6
  15.4 0.8 %shard_map.79.image = f32[2,16,128]{2,1,0:T(8,128)S(1)} custom-call(f32[6,32,128]{2,1,0:T(8,128)S(1)} %collective-permute-done.arrived, s32[32,16,128]{2,1,0:T(8,128)S(1)} %get-tuple-element.19.own0, f32[32,16,128]{2,1,0:T(8,128)S(1)} %get-tuple-element.20.own1, s32[32,16,128]{2,1,0:T(8,128)S(1)} %get-tuple-element.21.own2, ...), custom_call_target="tpu_custom_call" | custom-call | flops 20000000 | bytes 2000000 | tf_op jit(solution)/shard_map/pallas_call | solution.py:237
  16.1 0.4 %collective-permute-done.6.other = f32[16,128]{1,0:T(8,128)S(1)} collective-permute-done((f32[16,128]{1,0:T(8,128)S(1)}, f32[16,128]{1,0:T(8,128)S(1)}, u32[]{:S(2)}, u32[]{:S(2)}) %collective-permute-start.6) | collective-permute-done | bytes 8224 | tf_op jit(solution)/shard_map/ppermute | solution.py:315
  16.5 1.6 %collective-permute-start.7 = (f32[1,8,128]{2,1,0:T(8,128)S(1)}, f32[1,8,128]{2,1,0:T(8,128)S(1)}, u32[]{:S(2)}, u32[]{:S(2)}) collective-permute-start(f32[1,8,128]{2,1,0:T(8,128)S(1)} %get-tuple-element.26), channel_id=1, source_target_pairs={{0,2},{1,3},{2,0},{3,1},{4,6},{5,7},{6,4},{7,5},{8,10},{9,11},{10,... | collective-permute-start | bytes 12296 | tf_op jit(solution)/shard_map/ppermute | solution.py:315
  18.1 2.0 %collective-permute-done.7.refs_1_ = f32[1,8,128]{2,1,0:T(8,128)S(1)} collective-permute-done((f32[1,8,128]{2,1,0:T(8,128)S(1)}, f32[1,8,128]{2,1,0:T(8,128)S(1)}, u32[]{:S(2)}, u32[]{:S(2)}) %collective-permute-start.7) | collective-permute-done | bytes 4128 | tf_op jit(solution)/shard_map/ppermute | solution.py:315
  20.1 1.6 %collective-permute-start.8 = (f32[2,4,128]{2,1,0:T(4,128)S(1)}, f32[2,4,128]{2,1,0:T(4,128)S(1)}, u32[]{:S(2)}, u32[]{:S(2)}) collective-permute-start(f32[2,4,128]{2,1,0:T(4,128)S(1)} %get-tuple-element.28), channel_id=1, source_target_pairs={{0,1},{1,0},{2,3},{3,2},{4,5},{5,4},{6,7},{7,6},{8,9},{9,8},{10,11... | collective-permute-start | bytes 12296 | tf_op jit(solution)/shard_map/ppermute | solution.py:315
  21.7 2.0 %collective-permute-done.8.came = f32[2,4,128]{2,1,0:T(4,128)S(1)} collective-permute-done((f32[2,4,128]{2,1,0:T(4,128)S(1)}, f32[2,4,128]{2,1,0:T(4,128)S(1)}, u32[]{:S(2)}, u32[]{:S(2)}) %collective-permute-start.8) | collective-permute-done | bytes 4128 | tf_op jit(solution)/shard_map/ppermute | solution.py:315
  23.8 0.6 %shard_map.82 = f32[1,4,4,128]{3,2,1,0:T(4,128)} custom-call(f32[2,4,128]{2,1,0:T(4,128)S(1)} %get-tuple-element.27.keep, f32[2,4,128]{2,1,0:T(4,128)S(1)} %collective-permute-done.8.came), custom_call_target="tpu_custom_call" | custom-call | tf_op jit(solution)/shard_map/pallas_call | solution.py:304
  (5 shorter events, 0.0 us)
Async XLA Ops:
  0.0 7.2 %collective-permute-start.1 = (s32[32,16,128]{2,1,0:T(8,128)}, s32[32,16,128]{2,1,0:T(8,128)S(1)}, u32[]{:S(2)}, u32[]{:S(2)}) collective-permute-start(s32[32,16,128]{2,1,0:T(8,128)} %bitcast.11), channel_id=1, source_target_pairs={{0,4},{4,0},{8,12},{12,8},{16,20},{20,16},{24,28},{28,24},{1,5},{5... | collective-permute-start | bytes 786440 | tf_op jit(solution)/shard_map/ppermute | solution.py:315
  0.5 8.7 %collective-permute-start.2 = (f32[32,16,128]{2,1,0:T(8,128)}, f32[32,16,128]{2,1,0:T(8,128)S(1)}, u32[]{:S(2)}, u32[]{:S(2)}) collective-permute-start(f32[32,16,128]{2,1,0:T(8,128)} %bitcast.13), channel_id=1, source_target_pairs={{0,4},{4,0},{8,12},{12,8},{16,20},{20,16},{24,28},{28,24},{1,5},{5... | collective-permute-start | bytes 786440 | tf_op jit(solution)/shard_map/ppermute | solution.py:315
  0.5 8.6 %collective-permute-start.3 = (s32[32,16,128]{2,1,0:T(8,128)}, s32[32,16,128]{2,1,0:T(8,128)S(1)}, u32[]{:S(2)}, u32[]{:S(2)}) collective-permute-start(s32[32,16,128]{2,1,0:T(8,128)} %bitcast.15), channel_id=1, source_target_pairs={{0,4},{4,0},{8,12},{12,8},{16,20},{20,16},{24,28},{28,24},{1,5},{5... | collective-permute-start | bytes 786440 | tf_op jit(solution)/shard_map/ppermute | solution.py:315
  2.0 9.4 %collective-permute-start.5 = (f32[6,32,128]{2,1,0:T(8,128)S(1)}, f32[6,32,128]{2,1,0:T(8,128)S(1)}, u32[]{:S(2)}, u32[]{:S(2)}) collective-permute-start(f32[6,32,128]{2,1,0:T(8,128)S(1)} %get-tuple-element.23), channel_id=1, source_target_pairs={{0,16},{4,20},{8,24},{12,28},{16,0},{20,4},{24,8},{28,12},{1,17},{... | collective-permute-start | bytes 294920 | tf_op jit(solution)/shard_map/ppermute | solution.py:315
  5.6 7.2 %collective-permute-start.4 = (f32[6,32,128]{2,1,0:T(8,128)S(1)}, f32[6,32,128]{2,1,0:T(8,128)S(1)}, u32[]{:S(2)}, u32[]{:S(2)}) collective-permute-start(f32[6,32,128]{2,1,0:T(8,128)S(1)} %get-tuple-element.22), channel_id=1, source_target_pairs={{0,8},{4,12},{8,0},{12,4},{16,24},{20,28},{24,16},{28,20},{1,9},{5... | collective-permute-start | bytes 294920 | tf_op jit(solution)/shard_map/ppermute | solution.py:315
  7.2 7.3 %collective-permute-start = (f32[6,32,128]{2,1,0:T(8,128)S(1)}, f32[6,32,128]{2,1,0:T(8,128)S(1)}, u32[]{:S(2)}, u32[]{:S(2)}) collective-permute-start(f32[6,32,128]{2,1,0:T(8,128)S(1)} %get-tuple-element.17), channel_id=1, source_target_pairs={{0,24},{4,28},{8,16},{12,20},{16,8},{20,12},{24,0},{28,4},{1,25},{... | collective-permute-start | bytes 294920 | tf_op jit(solution)/shard_map/ppermute | solution.py:315
  15.3 1.2 %collective-permute-start.6 = (f32[16,128]{1,0:T(8,128)S(1)}, f32[16,128]{1,0:T(8,128)S(1)}, u32[]{:S(2)}, u32[]{:S(2)}) collective-permute-start(f32[16,128]{1,0:T(8,128)S(1)} %slice_bitcast_fusion), channel_id=1, source_target_pairs={{0,4},{4,0},{8,12},{12,8},{16,20},{20,16},{24,28},{28,24},{1,5},{5... | collective-permute-start | bytes 24584 | tf_op jit(solution)/shard_map/ppermute | solution.py:315
  16.5 3.6 %collective-permute-start.7 = (f32[1,8,128]{2,1,0:T(8,128)S(1)}, f32[1,8,128]{2,1,0:T(8,128)S(1)}, u32[]{:S(2)}, u32[]{:S(2)}) collective-permute-start(f32[1,8,128]{2,1,0:T(8,128)S(1)} %get-tuple-element.26), channel_id=1, source_target_pairs={{0,2},{1,3},{2,0},{3,1},{4,6},{5,7},{6,4},{7,5},{8,10},{9,11},{10,... | collective-permute-start | bytes 12296 | tf_op jit(solution)/shard_map/ppermute | solution.py:315
  20.1 3.6 %collective-permute-start.8 = (f32[2,4,128]{2,1,0:T(4,128)S(1)}, f32[2,4,128]{2,1,0:T(4,128)S(1)}, u32[]{:S(2)}, u32[]{:S(2)}) collective-permute-start(f32[2,4,128]{2,1,0:T(4,128)S(1)} %get-tuple-element.28), channel_id=1, source_target_pairs={{0,1},{1,0},{2,3},{3,2},{4,5},{5,4},{6,7},{7,6},{8,9},{9,8},{10,11... | collective-permute-start | bytes 12296 | tf_op jit(solution)/shard_map/ppermute | solution.py:315

commit v5 on v4

--- a/solution.py
+++ b/solution.py
@@ -137,28 +137,40 @@
     for j in range(capacity):
         live = live + (notes[(q * capacity + j) * each] > 0).astype(jnp.int32)
 
-    def add_slot(j, _):
-        slot = q * capacity + j
+    def contribution(slot, part):
+        total = None
         s = notes[slot * each] - 1
         for i in range(per_block):
             r = notes[slot * each + 1 + i]
-            for half in range(times.shape[1] // SUBLANES):
-                part = pl.ds(SUBLANES * half, SUBLANES)
-                t = times[s, part] + times[r, part]
-                c = jnp.maximum(widths[s, part], widths[r, part])
-                weight = amps[s, part] * amps[r, part]
-                within = t & (LANES - 1)
-                wanted = c * steps + (t >> 7)
-                total = None
-                for c in range(3):
-                    for h in range(steps):
-                        line = filtered[slot, c, pl.ds(per_block * h + i, 1), :]
-                        got = jnp.take_along_axis(jnp.broadcast_to(line, (SUBLANES, LANES)), within, axis=1)
-                        total = got if total is None else jnp.where(wanted == c * steps + h, got, total)
-                image[q, part] += weight * total
+            t = times[s, part] + times[r, part]
+            c = jnp.maximum(widths[s, part], widths[r, part])
+            weight = amps[s, part] * amps[r, part]
+            within = t & (LANES - 1)
+            wanted = c * steps + (t >> 7)
+            picked = None
+            for c in range(3):
+                for h in range(steps):
+                    line = filtered[slot, c, pl.ds(per_block * h + i, 1), :]
+                    got = jnp.take_along_axis(jnp.broadcast_to(line, (SUBLANES, LANES)), within, axis=1)
+                    picked = got if picked is None else jnp.where(wanted == c * steps + h, got, picked)
+            total = weight * picked if total is None else total + weight * picked
+        return total
+
+    def add(slots):
+        for half in range(times.shape[1] // SUBLANES):
+            part = pl.ds(SUBLANES * half, SUBLANES)
+            image[q, part] += sum(contribution(slot, part) for slot in slots)
+
+    def add_two(j, _):
+        add((q * capacity + 2 * j, q * capacity + 2 * j + 1))
         return 0
 
-    lax.fori_loop(0, live, add_slot, 0)
+    def add_last(j, _):
+        add((q * capacity + j,))
+        return 0
+
+    lax.fori_loop(0, live >> 1, add_two, 0)
+    lax.fori_loop(live & -2, live, add_last, 0)
 
 
 def read_notes(arrived, notes, per_block, samples, qs):
@@ -171,7 +183,7 @@
 
 
 def first_kernel(
-    qs, per_block, samples, arrived, own0, own1, own2, image, times, amps, widths, filtered, notes, sems,
+    qs, per_block, samples, arrived, own0, own1, own2, sib0, sib1, sib2, image, times, amps, widths, filtered, notes, sems,
 ):
     pairs = ((own0, times), (own1, amps), (own2, widths))
     loads = []
@@ -186,10 +198,10 @@
     image[...] = jnp.zeros(image.shape, jnp.float32)
     read_notes(arrived, notes, per_block, samples, qs)
     filter_slots(arrived, filtered, per_block, samples, qs)
+    add_slots(1, notes, filtered, (sib0, sib1, sib2), image, per_block, samples)
     for load in loads:
         load.wait()
-    for q in qs:
-        add_slots(q, notes, filtered, (times, amps, widths), image, per_block, samples)
+    add_slots(0, notes, filtered, (times, amps, widths), image, per_block, samples)
 
 
 def next_kernel(
@@ -217,19 +229,19 @@
     return [pltpu.with_memory_space_constraint(a, pltpu.HBM) for a in arrays]
 
 
-def migrate_first(arrived, own, qs, per_block, samples):
+def migrate_first(arrived, own, sibling, per_block, samples):
     pieces = math.gcd(own[0].shape[0], 4)
     shape = own[0].shape
     outs = pl.pallas_call(
-        functools.partial(first_kernel, qs, per_block, samples),
+        functools.partial(first_kernel, (1, 0), per_block, samples),
         out_shape=[jax.ShapeDtypeStruct((2,) + shape[1:], jnp.float32)]
         + [jax.ShapeDtypeStruct(t.shape, t.dtype) for t in own],
-        in_specs=[VMEM] + [HBM] * 3,
+        in_specs=[VMEM] + [HBM] * 3 + [VMEM] * 3,
         out_specs=[VMEM] * 4,
         scratch_shapes=migrate_scratch(arrived, per_block) + [pltpu.SemaphoreType.DMA((3 * pieces,))],
         compiler_params=PARAMS,
         cost_estimate=COST,
-    )(arrived, *in_hbm(*own))
+    )(arrived, *in_hbm(*own), *sibling)
     return outs[0], tuple(outs[1:4])
 
 
@@ -328,8 +340,7 @@
     packed = pack(src_node, rec_node[0].T, aperture[0].T, traces, chips, capacity)
     arrived = [packed[0]] + [swap_chips(packed[1 + n], n, chips) for n in range(chips - 1)]
     sibling = tuple(swap(t, "tile", 1) for t in own)
-    image, own = migrate_first(arrived[0], own, (0,), per_block, samples)
-    image = migrate(arrived[0], own, sibling, image, (1,), per_block, samples)
+    image, own = migrate_first(arrived[0], own, sibling, per_block, samples)
     image = migrate(arrived[1], own, sibling, image, (1, 0), per_block, samples)
     for k in range(2, chips - 1):
         image = migrate(arrived[k], own, sibling, image, (1, 0), per_block, samples)

time: 24.6 us -> 24.3 us (0.988)
  Pallas kernels: 8.76 us -> 6.94 us
  waiting for transfers between devices: 6.05 us -> 7.76 us
    pallas_call x5 -> x4, Pallas kernels: 5.23 us -> 3.39 us  [migrate(): pl.pallas_call(functools.partial(next_kernel, qs, per_block, samples), ou...]
    ppermute x9, waiting for transfers between devices: 6.05 us -> 7.76 us  [swap(): return lax.ppermute(value, axis, [(i, i ^ k) for i in range(size)])]
  transfers between devices with their start and end apart: 9 -> 9, of which waited for: 5 -> 5; matrix products, arithmetic and copies ran while one was open for 0% -> 0% of each run, Pallas kernels for 30% -> 24%
where the time goes in v5:
time: 24.3 us; the launch traced here: 24.1 us
  starting transfers between devices  9.28 us (38%)
  waiting for transfers between devices  7.76 us (32%)
  Pallas kernels  6.94 us (29%)
    ppermute x9, starting transfers between devices, swap(): return lax.ppermute(value, axis, [(i, i ^ k) for i in range(size)])  9.28 us
    ppermute x9, waiting for transfers between devices, swap(): return lax.ppermute(value, axis, [(i, i ^ k) for i in range(size)])  7.76 us
    pallas_call x4, Pallas kernels, migrate(): pl.pallas_call(functools.partial(next_kernel, qs, per_block, samples), ou...  3.39 us
    pallas_call x1, Pallas kernels, migrate_first(): pl.pallas_call(functools.partial(first_kernel, (1, 0), per_block, samples...  1.95 us
    pallas_call x1, Pallas kernels, pack(): pl.pallas_call(functools.partial(pack_kernel, chips, capacity), out_shape...  0.98 us
    pallas_call x1, Pallas kernels, exchange_slabs(): pl.pallas_call(functools.partial(gather_kernel, order), out_shape=jax.Sha...  0.61 us
  transfers between devices with their start and end apart: 9, of which 5 were waited for; matrix products, arithmetic and copies ran while one was open for 0% of the time, Pallas kernels for 24%

profile of v5, /device:TPU:0, one launch (start us, length us, event | category | flops | bytes accessed | tf_op | source)
XLA Modules:
  0.0 24.1 jit_solution(6998652892188640363)
XLA Ops:
  0.0 0.5 %collective-permute-start.1 = (s32[32,16,128]{2,1,0:T(8,128)}, s32[32,16,128]{2,1,0:T(8,128)S(1)}, u32[]{:S(2)}, u32[]{:S(2)}) collective-permute-start(s32[32,16,128]{2,1,0:T(8,128)} %bitcast.11), channel_id=1, source_target_pairs={{0,4},{4,0},{8,12},{12,8},{16,20},{20,16},{24,28},{28,24},{1,5},{5... | collective-permute-start | bytes 786440 | tf_op jit(solution)/shard_map/ppermute | solution.py:327
  0.5 0.1 collective-permute-start.2
  0.5 0.5 %collective-permute-start.3 = (s32[32,16,128]{2,1,0:T(8,128)}, s32[32,16,128]{2,1,0:T(8,128)S(1)}, u32[]{:S(2)}, u32[]{:S(2)}) collective-permute-start(s32[32,16,128]{2,1,0:T(8,128)} %bitcast.15), channel_id=1, source_target_pairs={{0,4},{4,0},{8,12},{12,8},{16,20},{20,16},{24,28},{28,24},{1,5},{5... | collective-permute-start | bytes 786440 | tf_op jit(solution)/shard_map/ppermute | solution.py:327
  1.0 1.0 %shard_map.73 = (f32[6,32,128]{2,1,0:T(8,128)S(1)}, f32[6,32,128]{2,1,0:T(8,128)S(1)}, f32[6,32,128]{2,1,0:T(8,128)S(1)}, f32[6,32,128]{2,1,0:T(8,128)S(1)}) custom-call(s32[1,8]{1,0:T(1,128)} %src_in.1, s32[2,8]{1,0:T(2,128)} %bitcast.17, s32[2,8]{1,0:T(2,128)} %bitcast.18, f32[1,8,2,2000]{3,2,1,0:T(2,128)} %traces_in.1), custom_call_target="tpu_custom_call" | custom-call | tf_op jit(solution)/shard_map/pallas_call | solution.py:81
  2.0 3.7 %collective-permute-start.5 = (f32[6,32,128]{2,1,0:T(8,128)S(1)}, f32[6,32,128]{2,1,0:T(8,128)S(1)}, u32[]{:S(2)}, u32[]{:S(2)}) collective-permute-start(f32[6,32,128]{2,1,0:T(8,128)S(1)} %get-tuple-element.23), channel_id=1, source_target_pairs={{0,16},{4,20},{8,24},{12,28},{16,0},{20,4},{24,8},{28,12},{1,17},{... | collective-permute-start | bytes 294920 | tf_op jit(solution)/shard_map/ppermute | solution.py:327
  5.6 1.6 %collective-permute-start.4 = (f32[6,32,128]{2,1,0:T(8,128)S(1)}, f32[6,32,128]{2,1,0:T(8,128)S(1)}, u32[]{:S(2)}, u32[]{:S(2)}) collective-permute-start(f32[6,32,128]{2,1,0:T(8,128)S(1)} %get-tuple-element.22), channel_id=1, source_target_pairs={{0,8},{4,12},{8,0},{12,4},{16,24},{20,28},{24,16},{28,20},{1,9},{5... | collective-permute-start | bytes 294920 | tf_op jit(solution)/shard_map/ppermute | solution.py:327
  7.2 0.0 collective-permute-done.1.sib0
  7.2 0.0 collective-permute-start
  7.2 0.0 collective-permute-done.2.sib1
  7.2 0.0 collective-permute-done.3.sib2
  7.2 2.0 %shard_map.74 = (f32[2,16,128]{2,1,0:T(8,128)S(1)}, s32[32,16,128]{2,1,0:T(8,128)S(1)}, f32[32,16,128]{2,1,0:T(8,128)S(1)}, s32[32,16,128]{2,1,0:T(8,128)S(1)}) custom-call(f32[6,32,128]{2,1,0:T(8,128)S(1)} %get-tuple-element.18.arrived, s32[32,16,128]{2,1,0:T(8,128)} %bitcast.12, f32[32,16,128]{2,1,0:T(8,128)} %bitcast.14, s32[32,16,128]{2,1,0:T(8,128)} %bitcast.16, ...), custom_call_target="tpu_custom_call" | custom-call | flops 20000000 | bytes 2000000 | tf_op jit(solution)/shard_map/pallas_call | solution.py:235
  9.2 2.2 %collective-permute-done.5.arrived = f32[6,32,128]{2,1,0:T(8,128)S(1)} collective-permute-done((f32[6,32,128]{2,1,0:T(8,128)S(1)}, f32[6,32,128]{2,1,0:T(8,128)S(1)}, u32[]{:S(2)}, u32[]{:S(2)}) %collective-permute-start.5) | collective-permute-done | bytes 98336 | tf_op jit(solution)/shard_map/ppermute | solution.py:327
  11.4 1.1 %shard_map.75.image_in = f32[2,16,128]{2,1,0:T(8,128)S(1)} custom-call(f32[6,32,128]{2,1,0:T(8,128)S(1)} %collective-permute-done.5.arrived, s32[32,16,128]{2,1,0:T(8,128)S(1)} %get-tuple-element.19.own0, f32[32,16,128]{2,1,0:T(8,128)S(1)} %get-tuple-element.20.own1, s32[32,16,128]{2,1,0:T(8,128)S(1)} %get-tuple-element.21.own2, ...), custom_call_target="tpu_custom_call" | custom-call | flops 20000000 | bytes 2000000 | tf_op jit(solution)/shard_map/pallas_call | solution.py:249
  12.5 1.1 %shard_map.76.image_in = f32[2,16,128]{2,1,0:T(8,128)S(1)} custom-call(f32[6,32,128]{2,1,0:T(8,128)S(1)} %collective-permute-done.4.arrived, s32[32,16,128]{2,1,0:T(8,128)S(1)} %get-tuple-element.19.own0, f32[32,16,128]{2,1,0:T(8,128)S(1)} %get-tuple-element.20.own1, s32[32,16,128]{2,1,0:T(8,128)S(1)} %get-tuple-element.21.own2, ...), custom_call_target="tpu_custom_call" | custom-call | flops 20000000 | bytes 2000000 | tf_op jit(solution)/shard_map/pallas_call | solution.py:249
  13.6 0.9 %collective-permute-done.arrived = f32[6,32,128]{2,1,0:T(8,128)S(1)} collective-permute-done((f32[6,32,128]{2,1,0:T(8,128)S(1)}, f32[6,32,128]{2,1,0:T(8,128)S(1)}, u32[]{:S(2)}, u32[]{:S(2)}) %collective-permute-start) | collective-permute-done | bytes 98336 | tf_op jit(solution)/shard_map/ppermute | solution.py:327
  14.5 0.5 %shard_map.77.image_in = f32[2,16,128]{2,1,0:T(8,128)S(1)} custom-call(f32[6,32,128]{2,1,0:T(8,128)S(1)} %collective-permute-done.arrived, s32[32,16,128]{2,1,0:T(8,128)S(1)} %get-tuple-element.19.own0, f32[32,16,128]{2,1,0:T(8,128)S(1)} %get-tuple-element.20.own1, s32[32,16,128]{2,1,0:T(8,128)S(1)} %get-tuple-element.21.own2, ...), custom_call_target="tpu_custom_call" | custom-call | flops 20000000 | bytes 2000000 | tf_op jit(solution)/shard_map/pallas_call | solution.py:249
  15.0 0.1 collective-permute-start.6
  15.1 0.7 %shard_map.78.image = f32[2,16,128]{2,1,0:T(8,128)S(1)} custom-call(f32[6,32,128]{2,1,0:T(8,128)S(1)} %collective-permute-done.arrived, s32[32,16,128]{2,1,0:T(8,128)S(1)} %get-tuple-element.19.own0, f32[32,16,128]{2,1,0:T(8,128)S(1)} %get-tuple-element.20.own1, s32[32,16,128]{2,1,0:T(8,128)S(1)} %get-tuple-element.21.own2, ...), custom_call_target="tpu_custom_call" | custom-call | flops 20000000 | bytes 2000000 | tf_op jit(solution)/shard_map/pallas_call | solution.py:249
  15.8 0.5 %collective-permute-done.6.other = f32[16,128]{1,0:T(8,128)S(1)} collective-permute-done((f32[16,128]{1,0:T(8,128)S(1)}, f32[16,128]{1,0:T(8,128)S(1)}, u32[]{:S(2)}, u32[]{:S(2)}) %collective-permute-start.6) | collective-permute-done | bytes 8224 | tf_op jit(solution)/shard_map/ppermute | solution.py:327
  16.2 1.5 %collective-permute-start.7 = (f32[1,8,128]{2,1,0:T(8,128)S(1)}, f32[1,8,128]{2,1,0:T(8,128)S(1)}, u32[]{:S(2)}, u32[]{:S(2)}) collective-permute-start(f32[1,8,128]{2,1,0:T(8,128)S(1)} %get-tuple-element.26), channel_id=1, source_target_pairs={{0,2},{1,3},{2,0},{3,1},{4,6},{5,7},{6,4},{7,5},{8,10},{9,11},{10,... | collective-permute-start | bytes 12296 | tf_op jit(solution)/shard_map/ppermute | solution.py:327
  17.8 2.1 %collective-permute-done.7.refs_1_ = f32[1,8,128]{2,1,0:T(8,128)S(1)} collective-permute-done((f32[1,8,128]{2,1,0:T(8,128)S(1)}, f32[1,8,128]{2,1,0:T(8,128)S(1)}, u32[]{:S(2)}, u32[]{:S(2)}) %collective-permute-start.7) | collective-permute-done | bytes 4128 | tf_op jit(solution)/shard_map/ppermute | solution.py:327
  19.9 1.5 %collective-permute-start.8 = (f32[2,4,128]{2,1,0:T(4,128)S(1)}, f32[2,4,128]{2,1,0:T(4,128)S(1)}, u32[]{:S(2)}, u32[]{:S(2)}) collective-permute-start(f32[2,4,128]{2,1,0:T(4,128)S(1)} %get-tuple-element.28), channel_id=1, source_target_pairs={{0,1},{1,0},{2,3},{3,2},{4,5},{5,4},{6,7},{7,6},{8,9},{9,8},{10,11... | collective-permute-start | bytes 12296 | tf_op jit(solution)/shard_map/ppermute | solution.py:327
  21.3 2.1 %collective-permute-done.8.came = f32[2,4,128]{2,1,0:T(4,128)S(1)} collective-permute-done((f32[2,4,128]{2,1,0:T(4,128)S(1)}, f32[2,4,128]{2,1,0:T(4,128)S(1)}, u32[]{:S(2)}, u32[]{:S(2)}) %collective-permute-start.8) | collective-permute-done | bytes 4128 | tf_op jit(solution)/shard_map/ppermute | solution.py:327
  23.5 0.6 %shard_map.81 = f32[1,4,4,128]{3,2,1,0:T(4,128)} custom-call(f32[2,4,128]{2,1,0:T(4,128)S(1)} %get-tuple-element.27.keep, f32[2,4,128]{2,1,0:T(4,128)S(1)} %collective-permute-done.8.came), custom_call_target="tpu_custom_call" | custom-call | tf_op jit(solution)/shard_map/pallas_call | solution.py:316
  (4 shorter events, 0.0 us)
Async XLA Ops:
  0.0 7.2 %collective-permute-start.1 = (s32[32,16,128]{2,1,0:T(8,128)}, s32[32,16,128]{2,1,0:T(8,128)S(1)}, u32[]{:S(2)}, u32[]{:S(2)}) collective-permute-start(s32[32,16,128]{2,1,0:T(8,128)} %bitcast.11), channel_id=1, source_target_pairs={{0,4},{4,0},{8,12},{12,8},{16,20},{20,16},{24,28},{28,24},{1,5},{5... | collective-permute-start | bytes 786440 | tf_op jit(solution)/shard_map/ppermute | solution.py:327
  0.5 6.7 %collective-permute-start.2 = (f32[32,16,128]{2,1,0:T(8,128)}, f32[32,16,128]{2,1,0:T(8,128)S(1)}, u32[]{:S(2)}, u32[]{:S(2)}) collective-permute-start(f32[32,16,128]{2,1,0:T(8,128)} %bitcast.13), channel_id=1, source_target_pairs={{0,4},{4,0},{8,12},{12,8},{16,20},{20,16},{24,28},{28,24},{1,5},{5... | collective-permute-start | bytes 786440 | tf_op jit(solution)/shard_map/ppermute | solution.py:327
  0.5 6.7 %collective-permute-start.3 = (s32[32,16,128]{2,1,0:T(8,128)}, s32[32,16,128]{2,1,0:T(8,128)S(1)}, u32[]{:S(2)}, u32[]{:S(2)}) collective-permute-start(s32[32,16,128]{2,1,0:T(8,128)} %bitcast.15), channel_id=1, source_target_pairs={{0,4},{4,0},{8,12},{12,8},{16,20},{20,16},{24,28},{28,24},{1,5},{5... | collective-permute-start | bytes 786440 | tf_op jit(solution)/shard_map/ppermute | solution.py:327
  2.0 9.4 %collective-permute-start.5 = (f32[6,32,128]{2,1,0:T(8,128)S(1)}, f32[6,32,128]{2,1,0:T(8,128)S(1)}, u32[]{:S(2)}, u32[]{:S(2)}) collective-permute-start(f32[6,32,128]{2,1,0:T(8,128)S(1)} %get-tuple-element.23), channel_id=1, source_target_pairs={{0,16},{4,20},{8,24},{12,28},{16,0},{20,4},{24,8},{28,12},{1,17},{... | collective-permute-start | bytes 294920 | tf_op jit(solution)/shard_map/ppermute | solution.py:327
  5.6 6.9 %collective-permute-start.4 = (f32[6,32,128]{2,1,0:T(8,128)S(1)}, f32[6,32,128]{2,1,0:T(8,128)S(1)}, u32[]{:S(2)}, u32[]{:S(2)}) collective-permute-start(f32[6,32,128]{2,1,0:T(8,128)S(1)} %get-tuple-element.22), channel_id=1, source_target_pairs={{0,8},{4,12},{8,0},{12,4},{16,24},{20,28},{24,16},{28,20},{1,9},{5... | collective-permute-start | bytes 294920 | tf_op jit(solution)/shard_map/ppermute | solution.py:327
  7.2 7.3 %collective-permute-start = (f32[6,32,128]{2,1,0:T(8,128)S(1)}, f32[6,32,128]{2,1,0:T(8,128)S(1)}, u32[]{:S(2)}, u32[]{:S(2)}) collective-permute-start(f32[6,32,128]{2,1,0:T(8,128)S(1)} %get-tuple-element.17), channel_id=1, source_target_pairs={{0,24},{4,28},{8,16},{12,20},{16,8},{20,12},{24,0},{28,4},{1,25},{... | collective-permute-start | bytes 294920 | tf_op jit(solution)/shard_map/ppermute | solution.py:327
  15.0 1.2 %collective-permute-start.6 = (f32[16,128]{1,0:T(8,128)S(1)}, f32[16,128]{1,0:T(8,128)S(1)}, u32[]{:S(2)}, u32[]{:S(2)}) collective-permute-start(f32[16,128]{1,0:T(8,128)S(1)} %slice_bitcast_fusion), channel_id=1, source_target_pairs={{0,4},{4,0},{8,12},{12,8},{16,20},{20,16},{24,28},{28,24},{1,5},{5... | collective-permute-start | bytes 24584 | tf_op jit(solution)/shard_map/ppermute | solution.py:327
  16.2 3.6 %collective-permute-start.7 = (f32[1,8,128]{2,1,0:T(8,128)S(1)}, f32[1,8,128]{2,1,0:T(8,128)S(1)}, u32[]{:S(2)}, u32[]{:S(2)}) collective-permute-start(f32[1,8,128]{2,1,0:T(8,128)S(1)} %get-tuple-element.26), channel_id=1, source_target_pairs={{0,2},{1,3},{2,0},{3,1},{4,6},{5,7},{6,4},{7,5},{8,10},{9,11},{10,... | collective-permute-start | bytes 12296 | tf_op jit(solution)/shard_map/ppermute | solution.py:327
  19.9 3.6 %collective-permute-start.8 = (f32[2,4,128]{2,1,0:T(4,128)S(1)}, f32[2,4,128]{2,1,0:T(4,128)S(1)}, u32[]{:S(2)}, u32[]{:S(2)}) collective-permute-start(f32[2,4,128]{2,1,0:T(4,128)S(1)} %get-tuple-element.28), channel_id=1, source_target_pairs={{0,1},{1,0},{2,3},{3,2},{4,5},{5,4},{6,7},{7,6},{8,9},{9,8},{10,11... | collective-permute-start | bytes 12296 | tf_op jit(solution)/shard_map/ppermute | solution.py:327

commit v6 on v5

--- a/solution.py
+++ b/solution.py
@@ -161,16 +161,17 @@
             part = pl.ds(SUBLANES * half, SUBLANES)
             image[q, part] += sum(contribution(slot, part) for slot in slots)
 
-    def add_two(j, _):
-        add((q * capacity + 2 * j, q * capacity + 2 * j + 1))
+    def add_all(j, _):
+        add([q * capacity + n for n in range(capacity)])
         return 0
 
-    def add_last(j, _):
+    def add_one(j, _):
         add((q * capacity + j,))
         return 0
 
-    lax.fori_loop(0, live >> 1, add_two, 0)
-    lax.fori_loop(live & -2, live, add_last, 0)
+    full = (live == capacity).astype(jnp.int32)
+    lax.fori_loop(0, full, add_all, 0)
+    lax.fori_loop(full * live, live, add_one, 0)
 
 
 def read_notes(arrived, notes, per_block, samples, qs):

time: 24.3 us -> 24.6 us (1.012)
  waiting for transfers between devices: 7.76 us -> 8.03 us
    ppermute x9, waiting for transfers between devices: 7.76 us -> 8.03 us  [swap(): return lax.ppermute(value, axis, [(i, i ^ k) for i in range(size)])]
  transfers between devices with their start and end apart: 9 -> 9, of which waited for: 5 -> 5; matrix products, arithmetic and copies ran while one was open for 0% -> 0% of each run, Pallas kernels for 24% -> 23%
where the time goes in v6:
time: 24.6 us; the launch traced here: 24.4 us
  starting transfers between devices  9.28 us (38%)
  waiting for transfers between devices  8.03 us (33%)
  Pallas kernels  6.96 us (28%)
    ppermute x9, starting transfers between devices, swap(): return lax.ppermute(value, axis, [(i, i ^ k) for i in range(size)])  9.28 us
    ppermute x9, waiting for transfers between devices, swap(): return lax.ppermute(value, axis, [(i, i ^ k) for i in range(size)])  8.03 us
    pallas_call x4, Pallas kernels, migrate(): pl.pallas_call(functools.partial(next_kernel, qs, per_block, samples), ou...  3.62 us
    pallas_call x1, Pallas kernels, migrate_first(): pl.pallas_call(functools.partial(first_kernel, (1, 0), per_block, samples...  1.74 us
    pallas_call x1, Pallas kernels, pack(): pl.pallas_call(functools.partial(pack_kernel, chips, capacity), out_shape...  0.98 us
    pallas_call x1, Pallas kernels, exchange_slabs(): pl.pallas_call(functools.partial(gather_kernel, order), out_shape=jax.Sha...  0.61 us
  transfers between devices with their start and end apart: 9, of which 5 were waited for; matrix products, arithmetic and copies ran while one was open for 0% of the time, Pallas kernels for 23%

profile of v6, /device:TPU:0, one launch (start us, length us, event | category | flops | bytes accessed | tf_op | source)
XLA Modules:
  0.0 24.4 jit_solution(2485301704396683434)
XLA Ops:
  0.0 0.5 %collective-permute-start.1 = (s32[32,16,128]{2,1,0:T(8,128)}, s32[32,16,128]{2,1,0:T(8,128)S(1)}, u32[]{:S(2)}, u32[]{:S(2)}) collective-permute-start(s32[32,16,128]{2,1,0:T(8,128)} %bitcast.11), channel_id=1, source_target_pairs={{0,4},{4,0},{8,12},{12,8},{16,20},{20,16},{24,28},{28,24},{1,5},{5... | collective-permute-start | bytes 786440 | tf_op jit(solution)/shard_map/ppermute | solution.py:328
  0.5 0.1 collective-permute-start.2
  0.5 0.5 %collective-permute-start.3 = (s32[32,16,128]{2,1,0:T(8,128)}, s32[32,16,128]{2,1,0:T(8,128)S(1)}, u32[]{:S(2)}, u32[]{:S(2)}) collective-permute-start(s32[32,16,128]{2,1,0:T(8,128)} %bitcast.15), channel_id=1, source_target_pairs={{0,4},{4,0},{8,12},{12,8},{16,20},{20,16},{24,28},{28,24},{1,5},{5... | collective-permute-start | bytes 786440 | tf_op jit(solution)/shard_map/ppermute | solution.py:328
  1.0 1.0 %shard_map.73 = (f32[6,32,128]{2,1,0:T(8,128)S(1)}, f32[6,32,128]{2,1,0:T(8,128)S(1)}, f32[6,32,128]{2,1,0:T(8,128)S(1)}, f32[6,32,128]{2,1,0:T(8,128)S(1)}) custom-call(s32[1,8]{1,0:T(1,128)} %src_in.1, s32[2,8]{1,0:T(2,128)} %bitcast.17, s32[2,8]{1,0:T(2,128)} %bitcast.18, f32[1,8,2,2000]{3,2,1,0:T(2,128)} %traces_in.1), custom_call_target="tpu_custom_call" | custom-call | tf_op jit(solution)/shard_map/pallas_call | solution.py:81
  2.0 3.7 %collective-permute-start.5 = (f32[6,32,128]{2,1,0:T(8,128)S(1)}, f32[6,32,128]{2,1,0:T(8,128)S(1)}, u32[]{:S(2)}, u32[]{:S(2)}) collective-permute-start(f32[6,32,128]{2,1,0:T(8,128)S(1)} %get-tuple-element.23), channel_id=1, source_target_pairs={{0,16},{4,20},{8,24},{12,28},{16,0},{20,4},{24,8},{28,12},{1,17},{... | collective-permute-start | bytes 294920 | tf_op jit(solution)/shard_map/ppermute | solution.py:328
  5.6 1.6 %collective-permute-start.4 = (f32[6,32,128]{2,1,0:T(8,128)S(1)}, f32[6,32,128]{2,1,0:T(8,128)S(1)}, u32[]{:S(2)}, u32[]{:S(2)}) collective-permute-start(f32[6,32,128]{2,1,0:T(8,128)S(1)} %get-tuple-element.22), channel_id=1, source_target_pairs={{0,8},{4,12},{8,0},{12,4},{16,24},{20,28},{24,16},{28,20},{1,9},{5... | collective-permute-start | bytes 294920 | tf_op jit(solution)/shard_map/ppermute | solution.py:328
  7.2 0.0 collective-permute-done.1.sib0
  7.2 0.0 collective-permute-start
  7.2 0.0 collective-permute-done.2.sib1
  7.2 0.0 collective-permute-done.3.sib2
  7.2 1.7 %shard_map.74 = (f32[2,16,128]{2,1,0:T(8,128)S(1)}, s32[32,16,128]{2,1,0:T(8,128)S(1)}, f32[32,16,128]{2,1,0:T(8,128)S(1)}, s32[32,16,128]{2,1,0:T(8,128)S(1)}) custom-call(f32[6,32,128]{2,1,0:T(8,128)S(1)} %get-tuple-element.18.arrived, s32[32,16,128]{2,1,0:T(8,128)} %bitcast.12, f32[32,16,128]{2,1,0:T(8,128)} %bitcast.14, s32[32,16,128]{2,1,0:T(8,128)} %bitcast.16, ...), custom_call_target="tpu_custom_call" | custom-call | flops 20000000 | bytes 2000000 | tf_op jit(solution)/shard_map/pallas_call | solution.py:236
  9.0 2.4 %collective-permute-done.5.arrived = f32[6,32,128]{2,1,0:T(8,128)S(1)} collective-permute-done((f32[6,32,128]{2,1,0:T(8,128)S(1)}, f32[6,32,128]{2,1,0:T(8,128)S(1)}, u32[]{:S(2)}, u32[]{:S(2)}) %collective-permute-start.5) | collective-permute-done | bytes 98336 | tf_op jit(solution)/shard_map/ppermute | solution.py:328
  11.4 1.2 %shard_map.75.image_in = f32[2,16,128]{2,1,0:T(8,128)S(1)} custom-call(f32[6,32,128]{2,1,0:T(8,128)S(1)} %collective-permute-done.5.arrived, s32[32,16,128]{2,1,0:T(8,128)S(1)} %get-tuple-element.19.own0, f32[32,16,128]{2,1,0:T(8,128)S(1)} %get-tuple-element.20.own1, s32[32,16,128]{2,1,0:T(8,128)S(1)} %get-tuple-element.21.own2, ...), custom_call_target="tpu_custom_call" | custom-call | flops 20000000 | bytes 2000000 | tf_op jit(solution)/shard_map/pallas_call | solution.py:250
  12.6 1.2 %shard_map.76.image_in = f32[2,16,128]{2,1,0:T(8,128)S(1)} custom-call(f32[6,32,128]{2,1,0:T(8,128)S(1)} %collective-permute-done.4.arrived, s32[32,16,128]{2,1,0:T(8,128)S(1)} %get-tuple-element.19.own0, f32[32,16,128]{2,1,0:T(8,128)S(1)} %get-tuple-element.20.own1, s32[32,16,128]{2,1,0:T(8,128)S(1)} %get-tuple-element.21.own2, ...), custom_call_target="tpu_custom_call" | custom-call | flops 20000000 | bytes 2000000 | tf_op jit(solution)/shard_map/pallas_call | solution.py:250
  13.8 0.7 %collective-permute-done.arrived = f32[6,32,128]{2,1,0:T(8,128)S(1)} collective-permute-done((f32[6,32,128]{2,1,0:T(8,128)S(1)}, f32[6,32,128]{2,1,0:T(8,128)S(1)}, u32[]{:S(2)}, u32[]{:S(2)}) %collective-permute-start) | collective-permute-done | bytes 98336 | tf_op jit(solution)/shard_map/ppermute | solution.py:328
  14.5 0.8 %shard_map.77.image_in = f32[2,16,128]{2,1,0:T(8,128)S(1)} custom-call(f32[6,32,128]{2,1,0:T(8,128)S(1)} %collective-permute-done.arrived, s32[32,16,128]{2,1,0:T(8,128)S(1)} %get-tuple-element.19.own0, f32[32,16,128]{2,1,0:T(8,128)S(1)} %get-tuple-element.20.own1, s32[32,16,128]{2,1,0:T(8,128)S(1)} %get-tuple-element.21.own2, ...), custom_call_target="tpu_custom_call" | custom-call | flops 20000000 | bytes 2000000 | tf_op jit(solution)/shard_map/pallas_call | solution.py:250
  15.3 0.1 collective-permute-start.6
  15.4 0.5 %shard_map.78.image = f32[2,16,128]{2,1,0:T(8,128)S(1)} custom-call(f32[6,32,128]{2,1,0:T(8,128)S(1)} %collective-permute-done.arrived, s32[32,16,128]{2,1,0:T(8,128)S(1)} %get-tuple-element.19.own0, f32[32,16,128]{2,1,0:T(8,128)S(1)} %get-tuple-element.20.own1, s32[32,16,128]{2,1,0:T(8,128)S(1)} %get-tuple-element.21.own2, ...), custom_call_target="tpu_custom_call" | custom-call | flops 20000000 | bytes 2000000 | tf_op jit(solution)/shard_map/pallas_call | solution.py:250
  15.9 0.7 %collective-permute-done.6.other = f32[16,128]{1,0:T(8,128)S(1)} collective-permute-done((f32[16,128]{1,0:T(8,128)S(1)}, f32[16,128]{1,0:T(8,128)S(1)}, u32[]{:S(2)}, u32[]{:S(2)}) %collective-permute-start.6) | collective-permute-done | bytes 8224 | tf_op jit(solution)/shard_map/ppermute | solution.py:328
  16.5 1.5 %collective-permute-start.7 = (f32[1,8,128]{2,1,0:T(8,128)S(1)}, f32[1,8,128]{2,1,0:T(8,128)S(1)}, u32[]{:S(2)}, u32[]{:S(2)}) collective-permute-start(f32[1,8,128]{2,1,0:T(8,128)S(1)} %get-tuple-element.26), channel_id=1, source_target_pairs={{0,2},{1,3},{2,0},{3,1},{4,6},{5,7},{6,4},{7,5},{8,10},{9,11},{10,... | collective-permute-start | bytes 12296 | tf_op jit(solution)/shard_map/ppermute | solution.py:328
  18.1 2.1 %collective-permute-done.7.refs_1_ = f32[1,8,128]{2,1,0:T(8,128)S(1)} collective-permute-done((f32[1,8,128]{2,1,0:T(8,128)S(1)}, f32[1,8,128]{2,1,0:T(8,128)S(1)}, u32[]{:S(2)}, u32[]{:S(2)}) %collective-permute-start.7) | collective-permute-done | bytes 4128 | tf_op jit(solution)/shard_map/ppermute | solution.py:328
  20.1 1.5 %collective-permute-start.8 = (f32[2,4,128]{2,1,0:T(4,128)S(1)}, f32[2,4,128]{2,1,0:T(4,128)S(1)}, u32[]{:S(2)}, u32[]{:S(2)}) collective-permute-start(f32[2,4,128]{2,1,0:T(4,128)S(1)} %get-tuple-element.28), channel_id=1, source_target_pairs={{0,1},{1,0},{2,3},{3,2},{4,5},{5,4},{6,7},{7,6},{8,9},{9,8},{10,11... | collective-permute-start | bytes 12296 | tf_op jit(solution)/shard_map/ppermute | solution.py:328
  21.6 2.1 %collective-permute-done.8.came = f32[2,4,128]{2,1,0:T(4,128)S(1)} collective-permute-done((f32[2,4,128]{2,1,0:T(4,128)S(1)}, f32[2,4,128]{2,1,0:T(4,128)S(1)}, u32[]{:S(2)}, u32[]{:S(2)}) %collective-permute-start.8) | collective-permute-done | bytes 4128 | tf_op jit(solution)/shard_map/ppermute | solution.py:328
  23.8 0.6 %shard_map.81 = f32[1,4,4,128]{3,2,1,0:T(4,128)} custom-call(f32[2,4,128]{2,1,0:T(4,128)S(1)} %get-tuple-element.27.keep, f32[2,4,128]{2,1,0:T(4,128)S(1)} %collective-permute-done.8.came), custom_call_target="tpu_custom_call" | custom-call | tf_op jit(solution)/shard_map/pallas_call | solution.py:317
  (4 shorter events, 0.0 us)
Async XLA Ops:
  0.0 7.2 %collective-permute-start.1 = (s32[32,16,128]{2,1,0:T(8,128)}, s32[32,16,128]{2,1,0:T(8,128)S(1)}, u32[]{:S(2)}, u32[]{:S(2)}) collective-permute-start(s32[32,16,128]{2,1,0:T(8,128)} %bitcast.11), channel_id=1, source_target_pairs={{0,4},{4,0},{8,12},{12,8},{16,20},{20,16},{24,28},{28,24},{1,5},{5... | collective-permute-start | bytes 786440 | tf_op jit(solution)/shard_map/ppermute | solution.py:328
  0.5 6.7 %collective-permute-start.2 = (f32[32,16,128]{2,1,0:T(8,128)}, f32[32,16,128]{2,1,0:T(8,128)S(1)}, u32[]{:S(2)}, u32[]{:S(2)}) collective-permute-start(f32[32,16,128]{2,1,0:T(8,128)} %bitcast.13), channel_id=1, source_target_pairs={{0,4},{4,0},{8,12},{12,8},{16,20},{20,16},{24,28},{28,24},{1,5},{5... | collective-permute-start | bytes 786440 | tf_op jit(solution)/shard_map/ppermute | solution.py:328
  0.5 6.7 %collective-permute-start.3 = (s32[32,16,128]{2,1,0:T(8,128)}, s32[32,16,128]{2,1,0:T(8,128)S(1)}, u32[]{:S(2)}, u32[]{:S(2)}) collective-permute-start(s32[32,16,128]{2,1,0:T(8,128)} %bitcast.15), channel_id=1, source_target_pairs={{0,4},{4,0},{8,12},{12,8},{16,20},{20,16},{24,28},{28,24},{1,5},{5... | collective-permute-start | bytes 786440 | tf_op jit(solution)/shard_map/ppermute | solution.py:328
  2.0 9.4 %collective-permute-start.5 = (f32[6,32,128]{2,1,0:T(8,128)S(1)}, f32[6,32,128]{2,1,0:T(8,128)S(1)}, u32[]{:S(2)}, u32[]{:S(2)}) collective-permute-start(f32[6,32,128]{2,1,0:T(8,128)S(1)} %get-tuple-element.23), channel_id=1, source_target_pairs={{0,16},{4,20},{8,24},{12,28},{16,0},{20,4},{24,8},{28,12},{1,17},{... | collective-permute-start | bytes 294920 | tf_op jit(solution)/shard_map/ppermute | solution.py:328
  5.6 7.0 %collective-permute-start.4 = (f32[6,32,128]{2,1,0:T(8,128)S(1)}, f32[6,32,128]{2,1,0:T(8,128)S(1)}, u32[]{:S(2)}, u32[]{:S(2)}) collective-permute-start(f32[6,32,128]{2,1,0:T(8,128)S(1)} %get-tuple-element.22), channel_id=1, source_target_pairs={{0,8},{4,12},{8,0},{12,4},{16,24},{20,28},{24,16},{28,20},{1,9},{5... | collective-permute-start | bytes 294920 | tf_op jit(solution)/shard_map/ppermute | solution.py:328
  7.2 7.3 %collective-permute-start = (f32[6,32,128]{2,1,0:T(8,128)S(1)}, f32[6,32,128]{2,1,0:T(8,128)S(1)}, u32[]{:S(2)}, u32[]{:S(2)}) collective-permute-start(f32[6,32,128]{2,1,0:T(8,128)S(1)} %get-tuple-element.17), channel_id=1, source_target_pairs={{0,24},{4,28},{8,16},{12,20},{16,8},{20,12},{24,0},{28,4},{1,25},{... | collective-permute-start | bytes 294920 | tf_op jit(solution)/shard_map/ppermute | solution.py:328
  15.3 1.2 %collective-permute-start.6 = (f32[16,128]{1,0:T(8,128)S(1)}, f32[16,128]{1,0:T(8,128)S(1)}, u32[]{:S(2)}, u32[]{:S(2)}) collective-permute-start(f32[16,128]{1,0:T(8,128)S(1)} %slice_bitcast_fusion), channel_id=1, source_target_pairs={{0,4},{4,0},{8,12},{12,8},{16,20},{20,16},{24,28},{28,24},{1,5},{5... | collective-permute-start | bytes 24584 | tf_op jit(solution)/shard_map/ppermute | solution.py:328
  16.5 3.6 %collective-permute-start.7 = (f32[1,8,128]{2,1,0:T(8,128)S(1)}, f32[1,8,128]{2,1,0:T(8,128)S(1)}, u32[]{:S(2)}, u32[]{:S(2)}) collective-permute-start(f32[1,8,128]{2,1,0:T(8,128)S(1)} %get-tuple-element.26), channel_id=1, source_target_pairs={{0,2},{1,3},{2,0},{3,1},{4,6},{5,7},{6,4},{7,5},{8,10},{9,11},{10,... | collective-permute-start | bytes 12296 | tf_op jit(solution)/shard_map/ppermute | solution.py:328
  20.1 3.6 %collective-permute-start.8 = (f32[2,4,128]{2,1,0:T(4,128)S(1)}, f32[2,4,128]{2,1,0:T(4,128)S(1)}, u32[]{:S(2)}, u32[]{:S(2)}) collective-permute-start(f32[2,4,128]{2,1,0:T(4,128)S(1)} %get-tuple-element.28), channel_id=1, source_target_pairs={{0,1},{1,0},{2,3},{3,2},{4,5},{5,4},{6,7},{7,6},{8,9},{9,8},{10,11... | collective-permute-start | bytes 12296 | tf_op jit(solution)/shard_map/ppermute | solution.py:328
